TPU v7x, 128 devices: a whole 4x4x4 slice. The times are simulated.
128 devices in a mesh: grp: 4 (over z_lo, core), leaf: 32 (over z_hi, y, x).
Axes of the slice: x: 4, y: 4, z: 4 (z_hi: 2, z_lo: 2; z = z_hi * 2 + z_lo), core: 2. Of those that a mesh axis runs over, the one named last changes fastest.
Arguments:
- matrix: bfloat16 [32768, 32768], P('grp', 'leaf'), may hold values from -0.0625 to 0.0625
- probes: bfloat16 [32768, 512], P('leaf'), may hold values from -6 to 6
- leaf_skeleton: int32 [128, 128], P(('grp', 'leaf')), may hold values from 0 to 255, as said below
- node_skeleton: int32 [127, 128], replicated, may hold values from 0 to 255, as said below
Outputs:
- leaf_basis: float32 [32768, 128], P(('grp', 'leaf'))
- transfer: float32 [128, 256, 128], P(('grp', 'leaf'))
Inputs may be any that keep to these rules, and one draw needn't show every extreme that they name: `leaf_skeleton`: each row holds 128 distinct increasing row numbers within one leaf. `node_skeleton`: each row holds 128 distinct increasing numbers into the node's stacked rows, the first child's 128 rows first.
All inputs are finite; a program needn't handle non-finite values.
Results may differ from a plain program's by a relative error of at most 0.0003.
Values sent between devices are 32-bit elements; how exact they have to be, the bound alone decides.
A program may use at most 128 MiB of HBM per device.

v0:
```python
import jax
import jax.numpy as jnp
from jax import lax
from jax.sharding import PartitionSpec as P


def from_partner(value, axis, stride):
    mask = 2**stride
    pairs = [(source, source ^ mask) for source in range(lax.axis_size(axis))]
    return lax.ppermute(value, axis, pairs)


def node_bases(stacked, picked):
    rows = jnp.take_along_axis(stacked, picked[:, :, None], axis=1)
    gram = jnp.einsum("nks,nls->nkl", rows, rows, precision=lax.Precision.HIGHEST)
    cross = jnp.einsum("nks,nis->nki", rows, stacked, precision=lax.Precision.HIGHEST)
    factor = jnp.linalg.cholesky(gram)
    first = lax.linalg.triangular_solve(factor, cross, left_side=True, lower=True)
    solved = lax.linalg.triangular_solve(
        factor, first, left_side=True, lower=True, transpose_a=True
    )
    return (jnp.swapaxes(solved, 1, 2), rows)


def on_device(matrix, probes, leaf_skeleton, node_skeleton):
    n_grp = lax.axis_size("grp")
    n_leaf = lax.axis_size("leaf")
    grp_pos = lax.axis_index("grp")
    leaf_pos = lax.axis_index("leaf")
    device = grp_pos * n_leaf + leaf_pos
    row_count, col_count = matrix.shape
    leaf_rows = row_count // n_leaf
    rank = leaf_skeleton.shape[1]
    all_leaves = n_grp * n_leaf
    leaf_bits = n_leaf.bit_length() - 1
    grp_bits = n_grp.bit_length() - 1
    levels = leaf_bits + grp_bits
    row_base = grp_pos * row_count
    col_leaf = (leaf_pos * col_count + jnp.arange(col_count, dtype=jnp.int32)) // leaf_rows
    row_index = jnp.arange(leaf_rows * lax.axis_size("leaf"), dtype=jnp.int32)
    block = jnp.take(matrix, row_index, axis=0)
    keep = ((row_base + row_index) // leaf_rows)[:, None] != col_leaf[None, :]
    block = jnp.where(keep, block, jnp.zeros((), matrix.dtype))
    samples_mine = lax.psum_scatter(
        jnp.dot(block, probes, preferred_element_type=jnp.float32),
        "leaf",
        scatter_dimension=0,
        tiled=True,
    )
    leaf_basis, carried = node_bases(samples_mine[None], leaf_skeleton)
    current = carried[0]
    result = jnp.zeros((2 * rank, rank), jnp.float32)

    def level_offset(level):
        total = 0
        for inner in range(1, level):
            total = total + (all_leaves >> inner)
        return total

    def keep_mine(result, level, basis):
        select = (device % (1 << level) == 1 << level - 1) | (device == 0) & (level == levels)
        return jnp.where(select, basis, result)

    def climb(current, partner, bit_value, level):
        lower = jnp.where(bit_value == 1, partner, current)
        upper = jnp.where(bit_value == 1, current, partner)
        stacked = jnp.concatenate([lower, upper], axis=0)[None]
        node = level_offset(level) + (device >> level)
        picked = lax.dynamic_slice_in_dim(node_skeleton, node, 1, 0)
        basis, rows = node_bases(stacked, picked)
        return (basis[0], rows[0])

    for bit in range(leaf_bits):
        partner = from_partner(current, "leaf", bit)
        basis, current = climb(current, partner, leaf_pos >> bit & 1, bit + 1)
        result = keep_mine(result, bit + 1, basis)
    for bit in range(grp_bits):
        partner = from_partner(current, "grp", bit)
        basis, current = climb(current, partner, grp_pos >> bit & 1, leaf_bits + bit + 1)
        result = keep_mine(result, leaf_bits + bit + 1, basis)
    return (leaf_basis[0], result[None])


def solution(mesh):
    return jax.shard_map(
        on_device,
        mesh=mesh,
        in_specs=(P("grp", "leaf"), P("leaf", None), P(("grp", "leaf"), None), P()),
        out_specs=(P(("grp", "leaf"), None), P(("grp", "leaf"), None, None)),
        check_vma=False,
    )
```

profile of v0, /device:TPU:0, one launch (start us, length us, event | category | flops | bytes accessed | tf_op | source)
XLA Modules:
  0.0 528.5 jit_solution(1492375444514211756)
XLA Ops:
  7.3 48.7 %gather_fusion = bf16[8192,1024]{1,0:T(8,128)(2,1)} fusion(bf16[8192,1024]{1,0:T(8,128)(2,1)} %param.11, s32[8192]{0:T(1024)S(1)} %iota_clamp_fusion), kind=kCustom, calls=%fused_computation.8 | custom fusion | bytes 33587200 | tf_op jit(solution)/shard_map/jit(_take)/gather | solution.py:41
  56.0 18.2 %fusion = f32[8192,512]{1,0:T(8,128)} fusion(bf16[1024,512]{1,0:T(8,128)(2,1)S(1)} %copy-done, bf16[8192,1024]{1,0:T(8,128)(2,1)} %gather_fusion, s32[1024]{0:T(1024)S(1)} %add_select_fusion.1, s32[8192]{0:T(1024)S(1)} %add_select_fusion, pred[8192]{0:T(1024)(128)(4,1)S(1)} %iota_compare_fusion.2), kind=kOutput, calls=%fused_computation.10 | convolution fusion | flops 8615100416 | bytes 34648064 | tf_op jit(solution)/shard_map/dot_general | solution.py:45
  74.3 0.9 fusion.94
  75.2 0.8 and_bitcast_fusion
  76.1 226.2 %reduce-scatter.2.cloned.1.call-done = f32[256,512]{1,0:T(8,128)} async-done(((f32[8192,512]{1,0:T(8,128)}), f32[256,512]{1,0:T(8,128)}) %reduce-scatter.2.cloned.1.call-update) | async-done | bytes 524304 | tf_op jit(solution)/shard_map/reduce_scatter | solution.py:44
  302.3 1.9 gather_fusion.1
  305.3 11.7 %custom-call.30 = f32[1,128,128]{2,1,0:T(8,128)S(1)} custom-call(f32[1,128,128]{2,1,0:T(8,128)S(1)} %fusion.45), custom_call_target="Cholesky" | custom-call | tf_op jit(solution)/shard_map/jit(cholesky)/cholesky | solution.py:17
  317.7 0.7 fusion.30
  318.4 9.8 %custom-call.32 = f32[1,1,128,128]{2,3,1,0:T(8,128)S(1)} custom-call(f32[1,1,128,128]{3,2,1,0:T(8,128)S(1)} %fusion.30), custom_call_target="InvertDiagBlocksLowerTriangular" | custom-call | tf_op jit(solution)/shard_map/triangular_solve/custom-call.2 | solution.py:19
  328.2 1.7 fusion.102
  330.5 0.8 copy.22
  331.4 0.8 gather_fusion.2
  332.3 0.7 fusion.100
  333.7 11.7 %custom-call.51 = f32[1,128,128]{2,1,0:T(8,128)S(1)} custom-call(f32[1,128,128]{2,1,0:T(8,128)S(1)} %fusion.38), custom_call_target="Cholesky" | custom-call | tf_op jit(solution)/shard_map/jit(cholesky)/cholesky | solution.py:17
  346.1 0.7 fusion.37
  346.8 9.8 %custom-call.53 = f32[1,1,128,128]{2,3,1,0:T(8,128)S(1)} custom-call(f32[1,1,128,128]{3,2,1,0:T(8,128)S(1)} %fusion.37), custom_call_target="InvertDiagBlocksLowerTriangular" | custom-call | tf_op jit(solution)/shard_map/triangular_solve/custom-call.2 | solution.py:19
  357.3 0.8 gather_fusion.3
  359.6 11.7 %custom-call.48 = f32[1,128,128]{2,1,0:T(8,128)S(1)} custom-call(f32[1,128,128]{2,1,0:T(8,128)S(1)} %fusion.39), custom_call_target="Cholesky" | custom-call | tf_op jit(solution)/shard_map/jit(cholesky)/cholesky | solution.py:17
  372.0 0.7 fusion.36
  372.7 9.8 %custom-call.50 = f32[1,1,128,128]{2,3,1,0:T(8,128)S(1)} custom-call(f32[1,1,128,128]{3,2,1,0:T(8,128)S(1)} %fusion.36), custom_call_target="InvertDiagBlocksLowerTriangular" | custom-call | tf_op jit(solution)/shard_map/triangular_solve/custom-call.2 | solution.py:19
  383.3 0.8 gather_fusion.4
  384.1 0.7 fusion.98
  385.2 4.4 collective-permute-start.3
  389.7 11.7 %custom-call.45 = f32[1,128,128]{2,1,0:T(8,128)S(1)} custom-call(f32[1,128,128]{2,1,0:T(8,128)S(1)} %fusion.40), custom_call_target="Cholesky" | custom-call | tf_op jit(solution)/shard_map/jit(cholesky)/cholesky | solution.py:17
  402.1 0.7 fusion.35
  402.8 9.8 %custom-call.47 = f32[1,1,128,128]{2,3,1,0:T(8,128)S(1)} custom-call(f32[1,1,128,128]{3,2,1,0:T(8,128)S(1)} %fusion.35), custom_call_target="InvertDiagBlocksLowerTriangular" | custom-call | tf_op jit(solution)/shard_map/triangular_solve/custom-call.2 | solution.py:19
  413.3 0.8 gather_fusion.5
  414.2 0.7 fusion.97
  415.2 4.3 collective-permute-start.4
  419.7 11.7 %custom-call.42 = f32[1,128,128]{2,1,0:T(8,128)S(1)} custom-call(f32[1,128,128]{2,1,0:T(8,128)S(1)} %fusion.41), custom_call_target="Cholesky" | custom-call | tf_op jit(solution)/shard_map/jit(cholesky)/cholesky | solution.py:17
  432.1 0.7 fusion.34
  432.7 9.8 %custom-call.44 = f32[1,1,128,128]{2,3,1,0:T(8,128)S(1)} custom-call(f32[1,1,128,128]{3,2,1,0:T(8,128)S(1)} %fusion.34), custom_call_target="InvertDiagBlocksLowerTriangular" | custom-call | tf_op jit(solution)/shard_map/triangular_solve/custom-call.2 | solution.py:19
  443.3 0.8 gather_fusion.6
  444.2 0.7 fusion.96
  445.6 11.7 %custom-call.39 = f32[1,128,128]{2,1,0:T(8,128)S(1)} custom-call(f32[1,128,128]{2,1,0:T(8,128)S(1)} %fusion.42), custom_call_target="Cholesky" | custom-call | tf_op jit(solution)/shard_map/jit(cholesky)/cholesky | solution.py:17
  458.0 0.7 fusion.33
  458.6 9.8 %custom-call.41 = f32[1,1,128,128]{2,3,1,0:T(8,128)S(1)} custom-call(f32[1,1,128,128]{3,2,1,0:T(8,128)S(1)} %fusion.33), custom_call_target="InvertDiagBlocksLowerTriangular" | custom-call | tf_op jit(solution)/shard_map/triangular_solve/custom-call.2 | solution.py:19
  469.2 0.8 gather_fusion.7
  470.1 0.7 fusion.95
  471.5 11.7 %custom-call.36 = f32[1,128,128]{2,1,0:T(8,128)S(1)} custom-call(f32[1,128,128]{2,1,0:T(8,128)S(1)} %fusion.43), custom_call_target="Cholesky" | custom-call | tf_op jit(solution)/shard_map/jit(cholesky)/cholesky | solution.py:17
  483.9 0.7 fusion.32
  484.6 9.8 %custom-call.38 = f32[1,1,128,128]{2,3,1,0:T(8,128)S(1)} custom-call(f32[1,1,128,128]{3,2,1,0:T(8,128)S(1)} %fusion.32), custom_call_target="InvertDiagBlocksLowerTriangular" | custom-call | tf_op jit(solution)/shard_map/triangular_solve/custom-call.2 | solution.py:19
  495.2 0.8 gather_fusion.8
  495.9 0.7 fusion.15
  497.2 11.7 %custom-call.33 = f32[1,128,128]{2,1,0:T(8,128)S(1)} custom-call(f32[1,128,128]{2,1,0:T(8,128)S(1)} %fusion.44), custom_call_target="Cholesky" | custom-call | tf_op jit(solution)/shard_map/jit(cholesky)/cholesky | solution.py:17
  509.6 0.7 fusion.31
  510.2 9.8 %custom-call.35 = f32[1,1,128,128]{2,3,1,0:T(8,128)S(1)} custom-call(f32[1,1,128,128]{3,2,1,0:T(8,128)S(1)} %fusion.31), custom_call_target="InvertDiagBlocksLowerTriangular" | custom-call | tf_op jit(solution)/shard_map/triangular_solve/custom-call.2 | solution.py:19
  520.6 0.8 copy.23
  (109 shorter events, 18.0 us)
Async XLA Ops:
  7.2 48.8 %copy-start = (bf16[1024,512]{1,0:T(8,128)(2,1)S(1)}, bf16[1024,512]{1,0:T(8,128)(2,1)}, u32[]{:S(2)}) copy-start(bf16[1024,512]{1,0:T(8,128)(2,1)} %param.12) | copy-start | bytes 3145732
  7.2 295.1 %reduce-scatter.2.cloned.1.call-start = ((), (), s32[]{:S(2)}) async-start(), calls=%async_computation.1 | async-start | bytes 17301504 | tf_op jit(solution)/shard_map/reduce_scatter | solution.py:44
  74.2 1.8 copy-start.2
  304.7 26.6 %collective-permute-start = (f32[128,512]{1,0:T(8,128)S(1)}, f32[128,512]{1,0:T(8,128)S(1)}, u32[]{:S(2)}, u32[]{:S(2)}) collective-permute-start(f32[128,512]{1,0:T(8,128)S(1)} %fusion.25), channel_id=1, source_target_pairs={{0,1},{1,0},{2,3},{3,2},{4,5},{5,4},{6,7},{7,6},{8,9},{9,8},{10,11... | collective-permute-start | bytes 786440 | tf_op jit(solution)/shard_map/ppermute | solution.py:10
  333.3 23.8 %collective-permute-start.1 = (f32[128,512]{1,0:T(8,128)S(1)}, f32[128,512]{1,0:T(8,128)S(1)}, u32[]{:S(2)}, u32[]{:S(2)}) collective-permute-start(f32[128,512]{1,0:T(8,128)S(1)} %fusion.24), channel_id=1, source_target_pairs={{0,2},{1,3},{2,0},{3,1},{4,6},{5,7},{6,4},{7,5},{8,10},{9,11},{10,... | collective-permute-start | bytes 786440 | tf_op jit(solution)/shard_map/ppermute | solution.py:10
  359.2 23.9 %collective-permute-start.2 = (f32[128,512]{1,0:T(8,128)S(1)}, f32[128,512]{1,0:T(8,128)S(1)}, u32[]{:S(2)}, u32[]{:S(2)}) collective-permute-start(f32[128,512]{1,0:T(8,128)S(1)} %fusion.23), channel_id=1, source_target_pairs={{0,4},{1,5},{2,6},{3,7},{4,0},{5,1},{6,2},{7,3},{8,12},{9,13},{10,... | collective-permute-start | bytes 786440 | tf_op jit(solution)/shard_map/ppermute | solution.py:10
  384.0 137.4 %copy-start.1 = (bf16[1024,512]{1,0:T(8,128)(2,1)S(1)}, bf16[1024,512]{1,0:T(8,128)(2,1)}, u32[]{:S(2)}) copy-start(bf16[1024,512]{1,0:T(8,128)(2,1)} %param.12) | copy-start | bytes 3145732
  385.2 28.0 %collective-permute-start.3 = (f32[128,512]{1,0:T(8,128)S(1)}, f32[128,512]{1,0:T(8,128)S(1)}, u32[]{:S(2)}, u32[]{:S(2)}) collective-permute-start(f32[128,512]{1,0:T(8,128)S(1)} %fusion.22), channel_id=1, source_target_pairs={{0,8},{1,9},{2,10},{3,11},{4,12},{5,13},{6,14},{7,15},{8,0},{9,1},... | collective-permute-start | bytes 786440 | tf_op jit(solution)/shard_map/ppermute | solution.py:10
  415.2 27.9 %collective-permute-start.4 = (f32[128,512]{1,0:T(8,128)S(1)}, f32[128,512]{1,0:T(8,128)S(1)}, u32[]{:S(2)}, u32[]{:S(2)}) collective-permute-start(f32[128,512]{1,0:T(8,128)S(1)} %fusion.21), channel_id=1, source_target_pairs={{0,16},{1,17},{2,18},{3,19},{4,20},{5,21},{6,22},{7,23},{8,24},{9,... | collective-permute-start | bytes 786440 | tf_op jit(solution)/shard_map/ppermute | solution.py:10
  445.2 23.8 %collective-permute-start.5 = (f32[128,512]{1,0:T(8,128)S(1)}, f32[128,512]{1,0:T(8,128)S(1)}, u32[]{:S(2)}, u32[]{:S(2)}) collective-permute-start(f32[128,512]{1,0:T(8,128)S(1)} %fusion.20), channel_id=1, source_target_pairs={{0,32},{32,0},{64,96},{96,64},{1,33},{33,1},{65,97},{97,65},{2,34}... | collective-permute-start | bytes 786440 | tf_op jit(solution)/shard_map/ppermute | solution.py:10
  471.1 23.9 %collective-permute-start.6 = (f32[128,512]{1,0:T(8,128)S(1)}, f32[128,512]{1,0:T(8,128)S(1)}, u32[]{:S(2)}, u32[]{:S(2)}) collective-permute-start(f32[128,512]{1,0:T(8,128)S(1)} %fusion.19), channel_id=1, source_target_pairs={{0,64},{32,96},{64,0},{96,32},{1,65},{33,97},{65,1},{97,33},{2,66}... | collective-permute-start | bytes 786440 | tf_op jit(solution)/shard_map/ppermute | solution.py:10
Sparse Core Ops, SparseCore 0:
  74.3 227.9 reduce-scatter.1
where the time goes:
time: 535 us; the launch traced here: 528 us
  waiting for transfers between devices  226 us (42%)
  other arithmetic  186 us (35%)
  local copies, waits for them, and re-layouts  58.1 us (11%)
  matrix products  32.2 us (6%)
  between operations  15.3 us (3%)
  starting transfers between devices  10.4 us (2%)
    reduce_scatter x1, waiting for transfers between devices, on_device(): lax.psum_scatter(jnp.dot(block, probes, preferred_element_type=jnp.float3...  226 us
    another operation x24, other arithmetic, node_bases(): factor = jnp.linalg.cholesky(gram)  99.1 us
    another operation x16, other arithmetic, node_bases(): lax.linalg.triangular_solve(factor, first, left_side=True, lower=True, tr...  83.7 us
    gather x1, local copies, waits for them, and re-layouts, on_device(): block = jnp.take(matrix, row_index, axis=0)  48.7 us
    dot_general x1, matrix products, on_device(): jnp.dot(block, probes, preferred_element_type=jnp.float32)  18.2 us
  transfers between devices with their start and end apart: 8, of which 1 were waited for; matrix products, arithmetic and copies ran while one was open for 32% of the time, Pallas kernels for 0%

commit v1 on v0

v1 whole, which is shorter than its diff:
```python
import jax
import jax.numpy as jnp
from jax import lax
from jax.sharding import PartitionSpec as P


def from_partner(value, axis, stride):
    mask = 2**stride
    pairs = [(source, source ^ mask) for source in range(lax.axis_size(axis))]
    return lax.ppermute(value, axis, pairs)


def node_bases(stacked, picked):
    rows = jnp.take_along_axis(stacked, picked[:, :, None], axis=1)
    gram = jnp.einsum("nks,nls->nkl", rows, rows, precision=lax.Precision.HIGHEST)
    cross = jnp.einsum("nks,nis->nki", rows, stacked, precision=lax.Precision.HIGHEST)
    factor = jnp.linalg.cholesky(gram)
    first = lax.linalg.triangular_solve(factor, cross, left_side=True, lower=True)
    solved = lax.linalg.triangular_solve(
        factor, first, left_side=True, lower=True, transpose_a=True
    )
    return jnp.swapaxes(solved, 1, 2)


def on_device(matrix, probes, leaf_skeleton, node_skeleton):
    n_grp = lax.axis_size("grp")
    n_leaf = lax.axis_size("leaf")
    grp_pos = lax.axis_index("grp")
    leaf_pos = lax.axis_index("leaf")
    device = grp_pos * n_leaf + leaf_pos
    row_count, col_count = matrix.shape
    leaf_rows = row_count // n_leaf
    rank = leaf_skeleton.shape[1]
    all_leaves = n_grp * n_leaf
    leaf_bits = n_leaf.bit_length() - 1
    grp_bits = n_grp.bit_length() - 1
    levels = leaf_bits + grp_bits
    row_leaf = grp_pos * n_leaf + jnp.arange(row_count, dtype=jnp.int32) // leaf_rows
    col_leaf = (leaf_pos * col_count + jnp.arange(col_count, dtype=jnp.int32)) // leaf_rows
    block = jnp.where(
        row_leaf[:, None] != col_leaf[None, :], matrix, jnp.zeros((), matrix.dtype)
    )
    samples_mine = lax.psum_scatter(
        jnp.dot(block, probes, preferred_element_type=jnp.float32),
        "leaf",
        scatter_dimension=0,
        tiled=True,
    )
    current = jnp.take(samples_mine, leaf_skeleton[0], axis=0)
    mine = jnp.zeros((2 * rank, samples_mine.shape[1]), jnp.float32)
    mine_picked = leaf_skeleton[0]
    offset = 0
    for level in range(1, levels + 1):
        if level <= leaf_bits:
            bit = leaf_pos >> (level - 1) & 1
            partner = from_partner(current, "leaf", level - 1)
        else:
            bit = grp_pos >> (level - 1 - leaf_bits) & 1
            partner = from_partner(current, "grp", level - 1 - leaf_bits)
        lower = jnp.where(bit == 1, partner, current)
        upper = jnp.where(bit == 1, current, partner)
        stacked = jnp.concatenate([lower, upper], axis=0)
        picked = node_skeleton[offset + (device >> level)]
        offset += all_leaves >> level
        select = (device % (1 << level) == 1 << level - 1) | (device == 0) & (level == levels)
        mine = jnp.where(select, stacked, mine)
        mine_picked = jnp.where(select, picked, mine_picked)
        if level < levels:
            current = jnp.take(stacked, picked, axis=0)
    bases = node_bases(
        jnp.stack([samples_mine, mine]), jnp.stack([leaf_skeleton[0], mine_picked])
    )
    return (bases[0], bases[1:])


def solution(mesh):
    return jax.shard_map(
        on_device,
        mesh=mesh,
        in_specs=(P("grp", "leaf"), P("leaf", None), P(("grp", "leaf"), None), P()),
        out_specs=(P(("grp", "leaf"), None), P(("grp", "leaf"), None, None)),
        check_vma=False,
    )
```

time: 535 us -> 373 us (0.70); the launches traced: 528 us -> 373 us
  other arithmetic: 186 us -> 51.2 us
  waiting for transfers between devices: 226 us -> 271 us
  local copies, waits for them, and re-layouts: 58.1 us -> 14.2 us
  matrix products: 32.2 us -> 19.8 us
  starting transfers between devices: 10.4 us -> 1.71 us
    another operation x24 -> x4, other arithmetic: 99.1 us -> 23.6 us  [node_bases(): factor = jnp.linalg.cholesky(gram)]
    another operation x16 -> x3, other arithmetic: 83.7 us -> 19.8 us  [node_bases(): lax.linalg.triangular_solve(factor, first, left_side=True, lower=True, tr...]
    ppermute x7, waiting for transfers between devices: 0.02 us -> 43.6 us  [from_partner(): return lax.ppermute(value, axis, pairs)]
    gather x1 -> x7, local copies, waits for them, and re-layouts: 48.7 us -> 6.45 us  [the longest x6 4.54 us: on_device(): current = jnp.take(stacked, picked, axis=0)]
    ppermute x7, starting transfers between devices: 10.4 us -> 1.67 us  [from_partner(): return lax.ppermute(value, axis, pairs)]
  transfers between devices with their start and end apart: 8 -> 8, of which waited for: 1 -> 8; matrix products, arithmetic and copies ran while one was open for 32% -> 0% of each run, Pallas kernels for 0% -> 0%
where the time goes in v1:
time: 373 us
  waiting for transfers between devices  271 us (73%)
  other arithmetic  51.2 us (14%)
  matrix products  19.8 us (5%)
  between operations  14.5 us (4%)
  local copies, waits for them, and re-layouts  14.2 us (4%)
    reduce_scatter x1, waiting for transfers between devices, on_device(): lax.psum_scatter(jnp.dot(block, probes, preferred_element_type=jnp.float3...  228 us
    ppermute x7, waiting for transfers between devices, from_partner(): return lax.ppermute(value, axis, pairs)  43.6 us
    another operation x4, other arithmetic, node_bases(): factor = jnp.linalg.cholesky(gram)  23.6 us
    another operation x3, other arithmetic, node_bases(): lax.linalg.triangular_solve(factor, first, left_side=True, lower=True, tr...  19.8 us
    dot_general x1, matrix products, on_device(): jnp.dot(block, probes, preferred_element_type=jnp.float32)  15.8 us
  transfers between devices with their start and end apart: 8, of which 8 were waited for; matrix products, arithmetic and copies ran while one was open for 0% of the time, Pallas kernels for 0%

profile of v1, /device:TPU:0, one launch (start us, length us, event | category | flops | bytes accessed | tf_op | source)
XLA Modules:
  0.0 372.9 jit_solution(5681043493496256687)
XLA Ops:
  7.3 1.1 copy-done
  8.4 15.8 %fusion = f32[8192,512]{1,0:T(8,128)} fusion(bf16[1024,512]{1,0:T(8,128)(2,1)S(1)} %copy-done, bf16[8192,1024]{1,0:T(8,128)(2,1)} %param.6, s32[1024]{0:T(1024)S(1)} %add_select_fusion.1, s32[8192]{0:T(1024)S(1)} %fusion.17), kind=kOutput, calls=%fused_computation.9 | convolution fusion | flops 8606711808 | bytes 34639872 | tf_op jit(solution)/shard_map/dot_general | solution.py:44
  24.2 0.6 copy-done.9
  24.9 227.8 %reduce-scatter.2.cloned.1.call-done = f32[256,512]{1,0:T(8,128)} async-done(((f32[8192,512]{1,0:T(8,128)}), f32[256,512]{1,0:T(8,128)}) %reduce-scatter.2.cloned.1.call-update) | async-done | bytes 524304 | tf_op jit(solution)/shard_map/reduce_scatter | solution.py:43
  252.7 1.9 gather_fusion.1
  254.8 0.8 compare_and_fusion
  255.6 5.5 %collective-permute-done = f32[128,512]{1,0:T(8,128)S(1)} collective-permute-done((f32[128,512]{1,0:T(8,128)S(1)}, f32[128,512]{1,0:T(8,128)S(1)}, u32[]{:S(2)}, u32[]{:S(2)}) %collective-permute-start) | collective-permute-done | bytes 262176 | tf_op jit(solution)/shard_map/ppermute | solution.py:10
  261.1 0.1 broadcast_select_fusion.8
  261.3 0.8 gather_fusion.2
  262.3 7.8 %collective-permute-done.1 = f32[128,512]{1,0:T(8,128)S(1)} collective-permute-done((f32[128,512]{1,0:T(8,128)S(1)}, f32[128,512]{1,0:T(8,128)S(1)}, u32[]{:S(2)}, u32[]{:S(2)}) %collective-permute-start.1) | collective-permute-done | bytes 262176 | tf_op jit(solution)/shard_map/ppermute | solution.py:10
  270.1 0.1 broadcast_select_fusion.10
  270.3 0.8 gather_fusion.3
  271.2 6.3 %collective-permute-done.2 = f32[128,512]{1,0:T(8,128)S(1)} collective-permute-done((f32[128,512]{1,0:T(8,128)S(1)}, f32[128,512]{1,0:T(8,128)S(1)}, u32[]{:S(2)}, u32[]{:S(2)}) %collective-permute-start.2) | collective-permute-done | bytes 262176 | tf_op jit(solution)/shard_map/ppermute | solution.py:10
  277.6 0.9 broadcast_select_fusion.12
  278.5 1.1 pad_maximum_fusion.3
  279.5 0.8 gather_fusion.4
  280.5 7.8 %collective-permute-done.3 = f32[128,512]{1,0:T(8,128)S(1)} collective-permute-done((f32[128,512]{1,0:T(8,128)S(1)}, f32[128,512]{1,0:T(8,128)S(1)}, u32[]{:S(2)}, u32[]{:S(2)}) %collective-permute-start.3) | collective-permute-done | bytes 262176 | tf_op jit(solution)/shard_map/ppermute | solution.py:10
  288.3 0.1 broadcast_select_fusion.14
  288.5 0.7 copy-done.3
  289.1 0.1 copy-done.4
  289.3 0.8 gather_fusion.5
  290.2 0.5 collective-permute-start.4
  290.7 7.4 %collective-permute-done.4 = f32[128,512]{1,0:T(8,128)S(1)} collective-permute-done((f32[128,512]{1,0:T(8,128)S(1)}, f32[128,512]{1,0:T(8,128)S(1)}, u32[]{:S(2)}, u32[]{:S(2)}) %collective-permute-start.4) | collective-permute-done | bytes 262176 | tf_op jit(solution)/shard_map/ppermute | solution.py:10
  298.1 0.1 broadcast_select_fusion.16
  298.3 0.7 copy-done.5
  299.1 0.8 gather_fusion.6
  299.8 0.8 broadcast_select_fusion.1
  300.6 0.8 broadcast_select_fusion.25
  301.5 0.9 collective-permute-done.5
  302.4 0.1 broadcast_select_fusion.18
  302.5 0.7 copy-done.7
  303.3 0.8 gather_fusion.7
  304.2 0.8 collective-permute-start.6
  305.0 7.7 %collective-permute-done.6 = f32[128,512]{1,0:T(8,128)S(1)} collective-permute-done((f32[128,512]{1,0:T(8,128)S(1)}, f32[128,512]{1,0:T(8,128)S(1)}, u32[]{:S(2)}, u32[]{:S(2)}) %collective-permute-start.6) | collective-permute-done | bytes 262176 | tf_op jit(solution)/shard_map/ppermute | solution.py:10
  312.8 0.1 select_bitcast_fusion.1
  312.9 2.0 maximum_select_fusion
  314.9 0.1 pad_maximum_fusion
  315.0 0.7 copy-done.2
  315.6 2.1 gather_fusion
  317.7 2.3 fusion.4
  320.0 0.8 fusion.6
  320.8 0.1 copy.8
  320.9 23.5 %custom-call.9 = f32[2,128,128]{2,1,0:T(8,128)S(1)} custom-call(f32[2,128,128]{2,1,0:T(8,128)S(1)} %fusion.16), custom_call_target="Cholesky" | custom-call | tf_op jit(solution)/shard_map/jit(cholesky)/cholesky | solution.py:17
  344.4 0.1 compare_reduce_fusion
  344.6 19.7 %custom-call.10 = f32[2,1,128,128]{2,3,1,0:T(8,128)S(1)} custom-call(f32[2,1,128,128]{3,2,1,0:T(8,128)S(1)} %select_bitcast_fusion.2), custom_call_target="InvertDiagBlocksLowerTriangular" | custom-call | tf_op jit(solution)/shard_map/triangular_solve | solution.py:19
  364.3 0.6 fusion.14
  364.9 0.4 fusion.12
  365.3 0.7 fusion.30
  (49 shorter events, 1.6 us)
Async XLA Ops:
  7.2 1.2 copy-start
  7.2 245.5 %reduce-scatter.2.cloned.1.call-start = ((), (), s32[]{:S(2)}) async-start(), calls=%async_computation.1 | async-start | bytes 17301504 | tf_op jit(solution)/shard_map/reduce_scatter | solution.py:43
  24.2 0.7 copy-start.9
  254.7 6.5 %collective-permute-start = (f32[128,512]{1,0:T(8,128)S(1)}, f32[128,512]{1,0:T(8,128)S(1)}, u32[]{:S(2)}, u32[]{:S(2)}) collective-permute-start(f32[128,512]{1,0:T(8,128)S(1)} %broadcast_select_fusion.6), channel_id=1, source_target_pairs={{0,1},{1,0},{2,3},{3,2},{4,5},{5,4},{6,7},{7,6},{8,9},{9,8},{10,11... | collective-permute-start | bytes 786440 | tf_op jit(solution)/shard_map/ppermute | solution.py:10
  261.3 53.6 %copy-start.1 = (f32[256,512]{1,0:T(8,128)S(1)}, f32[256,512]{1,0:T(8,128)}, u32[]{:S(2)}) copy-start(f32[256,512]{1,0:T(8,128)} %reduce-scatter.2.cloned.1.call-done) | copy-start | bytes 1572868
  262.2 8.0 %collective-permute-start.1 = (f32[128,512]{1,0:T(8,128)S(1)}, f32[128,512]{1,0:T(8,128)S(1)}, u32[]{:S(2)}, u32[]{:S(2)}) collective-permute-start(f32[128,512]{1,0:T(8,128)S(1)} %broadcast_select_fusion.5), channel_id=1, source_target_pairs={{0,2},{1,3},{2,0},{3,1},{4,6},{5,7},{6,4},{7,5},{8,10},{9,11},{10,... | collective-permute-start | bytes 786440 | tf_op jit(solution)/shard_map/ppermute | solution.py:10
  271.1 6.5 %collective-permute-start.2 = (f32[128,512]{1,0:T(8,128)S(1)}, f32[128,512]{1,0:T(8,128)S(1)}, u32[]{:S(2)}, u32[]{:S(2)}) collective-permute-start(f32[128,512]{1,0:T(8,128)S(1)} %broadcast_select_fusion.4), channel_id=1, source_target_pairs={{0,4},{1,5},{2,6},{3,7},{4,0},{5,1},{6,2},{7,3},{8,12},{9,13},{10,... | collective-permute-start | bytes 786440 | tf_op jit(solution)/shard_map/ppermute | solution.py:10
  280.4 8.0 %collective-permute-start.3 = (f32[128,512]{1,0:T(8,128)S(1)}, f32[128,512]{1,0:T(8,128)S(1)}, u32[]{:S(2)}, u32[]{:S(2)}) collective-permute-start(f32[128,512]{1,0:T(8,128)S(1)} %broadcast_select_fusion.3), channel_id=1, source_target_pairs={{0,8},{1,9},{2,10},{3,11},{4,12},{5,13},{6,14},{7,15},{8,0},{9,1},... | collective-permute-start | bytes 786440 | tf_op jit(solution)/shard_map/ppermute | solution.py:10
  288.4 0.7 copy-start.3
  288.5 0.8 copy-start.4
  290.2 8.0 %collective-permute-start.4 = (f32[128,512]{1,0:T(8,128)S(1)}, f32[128,512]{1,0:T(8,128)S(1)}, u32[]{:S(2)}, u32[]{:S(2)}) collective-permute-start(f32[128,512]{1,0:T(8,128)S(1)} %broadcast_select_fusion.2), channel_id=1, source_target_pairs={{0,16},{1,17},{2,18},{3,19},{4,20},{5,21},{6,22},{7,23},{8,24},{9,... | collective-permute-start | bytes 786440 | tf_op jit(solution)/shard_map/ppermute | solution.py:10
  298.2 0.7 copy-start.5
  298.2 0.8 copy-start.6
  300.6 1.7 collective-permute-start.5
  302.5 0.7 copy-start.7
  302.5 0.8 copy-start.8
  304.2 8.6 %collective-permute-start.6 = (f32[128,512]{1,0:T(8,128)S(1)}, f32[128,512]{1,0:T(8,128)S(1)}, u32[]{:S(2)}, u32[]{:S(2)}) collective-permute-start(f32[128,512]{1,0:T(8,128)S(1)} %broadcast_select_fusion), channel_id=1, source_target_pairs={{0,64},{32,96},{64,0},{96,32},{1,65},{33,97},{65,1},{97,33},{2,66}... | collective-permute-start | bytes 786440 | tf_op jit(solution)/shard_map/ppermute | solution.py:10
  314.8 0.8 copy-start.2
Sparse Core Ops, SparseCore 0:
  24.4 228.2 reduce-scatter.1

commit v2 on v1

--- a/solution.py
+++ b/solution.py
@@ -1,7 +1,381 @@
 import jax
 import jax.numpy as jnp
 from jax import lax
+from jax.experimental import pallas as pl
+from jax.experimental.pallas import tpu as pltpu
 from jax.sharding import PartitionSpec as P
+
+NX, NY, NZ = 4, 4, 2
+LR = 256
+RANK = 128
+HALF = 256
+SLOTS = 8
+CHUNKS = ((0, 128), (128, 128))
+F32 = jnp.float32
+BF16 = jnp.bfloat16
+ORDER = (
+    [(2, 0), (2, 1), (2, 2), (2, 3)]
+    + [(0, 2), (1, 2), (3, 2)]
+    + [(1, 0), (1, 1), (1, 3)]
+    + [(3, 0), (3, 1), (3, 3)]
+    + [(0, 1), (0, 3), (0, 0)]
+)
+OPP_R, OPP_L, NEAR_RA, NEAR_RB, NEAR_LA, NEAR_LB = range(6)
+PASS = 6
+Z_COPY = 2 * PASS
+N_COPY = 2 * PASS + 1
+
+
+def mod4(v):
+    return lax.rem(v + 4, 4)
+
+
+class Half:
+    def __init__(self, part, bufs, zbuf, send, recv, rows, first, second, zh, dev):
+        self.part, self.bufs, self.zbuf = part, bufs, zbuf
+        self.send, self.recv = send, recv
+        self.rows = rows
+        self.axes = (first, second)
+        self.zh = zh
+        self.dev = dev
+        self.started = []
+
+    def block(self, phase, index):
+        if phase == 0:
+            return self.part.at[index]
+        return self.part.at[self.axes[0][1], index]
+
+    def copy(self, phase, kind):
+        name, me = self.axes[phase]
+        half = self.rows // 2
+        opp, near_r, near_l = self.bufs[phase]
+        lo, hi = pl.ds(0, half), pl.ds(half, half)
+        lead = (slice(None),) * (2 if phase == 0 else 1)
+        right, left = mod4(me + 1), mod4(me - 1)
+        index, rows, dst, to = {
+            OPP_R: (mod4(me + 2), lo, opp.at[0], right),
+            OPP_L: (mod4(me + 2), hi, opp.at[1], left),
+            NEAR_RA: (right, lo, near_r.at[(*lead, lo)], right),
+            NEAR_RB: (right, hi, near_r.at[(*lead, hi)], right),
+            NEAR_LA: (left, lo, near_l.at[(*lead, lo)], left),
+            NEAR_LB: (left, hi, near_l.at[(*lead, hi)], left),
+        }[kind]
+        slot = phase * PASS + kind
+        return pltpu.make_async_remote_copy(
+            src_ref=self.block(phase, index).at[(*lead, rows)],
+            dst_ref=dst,
+            send_sem=self.send.at[slot],
+            recv_sem=self.recv.at[slot],
+            device_id=self.dev(**{name: to}),
+            device_id_type=pl.DeviceIdType.MESH,
+        )
+
+    def start(self, phase, *kinds):
+        for kind in kinds:
+            copy = self.copy(phase, kind)
+            copy.start()
+            self.started.append(copy)
+
+    def wait(self, phase, kind):
+        self.copy(phase, kind).wait_recv()
+
+    def relay(self, phase):
+        me = self.axes[phase][1]
+        half = self.rows // 2
+        opp = self.bufs[phase][0]
+        for kind, side, index, row, on in (
+            (OPP_R, 0, mod4(me + 1), 0, NEAR_RA),
+            (OPP_L, 1, mod4(me - 1), half, NEAR_LB),
+        ):
+            self.wait(phase, kind)
+            self.add(phase, index, row, half, (opp.at[side],), 0)
+            self.start(phase, on)
+
+    def gather(self, phase):
+        me = self.axes[phase][1]
+        for kind in (NEAR_RB, NEAR_LA, NEAR_RA, NEAR_LB):
+            self.wait(phase, kind)
+        self.add(phase, me, 0, self.rows, self.bufs[phase][1:], 0)
+
+    def add(self, phase, index, row, count, terms, term_row):
+        target = self.block(phase, index)
+        rows, term_rows = pl.ds(row, count), pl.ds(term_row, count)
+        if phase == 0:
+
+            def step(i, carry):
+                at = (i // NZ, lax.rem(i, NZ))
+                value = target[(*at, rows)]
+                for term in terms:
+                    value = value + term[(*at, term_rows)]
+                target[(*at, rows)] = value
+                return carry
+
+            lax.fori_loop(0, 4 * NZ, step, 0)
+        else:
+            for z in range(NZ):
+                value = target[z, rows]
+                for term in terms:
+                    value = value + term[z, term_rows]
+                target[z, rows] = value
+
+    def z_copy(self):
+        return pltpu.make_async_remote_copy(
+            src_ref=self.part.at[self.axes[0][1], self.axes[1][1], 1 - self.zh],
+            dst_ref=self.zbuf,
+            send_sem=self.send.at[Z_COPY],
+            recv_sem=self.recv.at[Z_COPY],
+            device_id=self.dev(z=1 - self.zh),
+            device_id_type=pl.DeviceIdType.MESH,
+        )
+
+    def z_start(self):
+        copy = self.z_copy()
+        copy.start()
+        self.started.append(copy)
+
+    def z_finish(self):
+        self.z_copy().wait_recv()
+        return self.part[self.axes[0][1], self.axes[1][1], self.zh] + self.zbuf[...]
+
+
+def leaf_order(skel):
+    hit = (lax.broadcasted_iota(jnp.int32, (LR, RANK), 0) == skel).astype(F32).astype(BF16)
+    picked = lax.dot_general(
+        jnp.ones((8, RANK), BF16), hit, (((1,), (1,)), ((), ())), preferred_element_type=F32
+    )
+    before = (
+        (
+            lax.broadcasted_iota(jnp.int32, (LR, LR), 0)
+            < lax.broadcasted_iota(jnp.int32, (LR, LR), 1)
+        )
+        .astype(F32)
+        .astype(BF16)
+    )
+    count = jnp.dot(picked.astype(BF16), before, preferred_element_type=F32)
+    lane = lax.broadcasted_iota(jnp.int32, (8, LR), 1).astype(F32)
+    place = jnp.where(picked > 0.5, count, RANK + lane - count)
+    return place[0:1]
+
+
+def kernel(
+    matrix,
+    probes,
+    skel,
+    out,
+    order_out,
+    slots,
+    permuted,
+    places,
+    in_sem,
+    place_send,
+    place_recv,
+    send,
+    recv,
+    *rest,
+):
+    leaf = lax.axis_index("leaf")
+    grp = lax.axis_index("grp")
+    x = lax.rem(leaf, NX)
+    y = lax.rem(leaf // NX, NY)
+    zh = leaf // (NX * NY)
+
+    def dev(x=x, y=y, z=zh):
+        return {"leaf": (z * NY + y) * NX + x}
+
+    barrier = pltpu.get_barrier_semaphore()
+    peers = [dev(x=mod4(x + k)) for k in (1, 2, 3)]
+    peers += [dev(y=mod4(y + k)) for k in (1, 2, 3)]
+    peers += [dev(z=1 - zh)]
+    for peer in peers:
+        pl.semaphore_signal(barrier, 1, device_id=peer, device_id_type=pl.DeviceIdType.MESH)
+
+    def place_of(t):
+        pair = t // NZ
+        i = sum(jnp.where(pair == k, o[0], 0) for k, o in enumerate(ORDER))
+        j = sum(jnp.where(pair == k, o[1], 0) for k, o in enumerate(ORDER))
+        return mod4(x + i), mod4(y + j), lax.rem(t, NZ)
+
+    def load(t):
+        xd, yd, zd = place_of(t)
+        dest = (zd * NY + yd) * NX + xd
+        slot = lax.rem(t, SLOTS)
+        return pltpu.make_async_copy(
+            matrix.at[pl.ds(pl.multiple_of(dest * LR, LR), LR), :],
+            slots.at[slot],
+            in_sem.at[slot],
+        )
+
+    def prefetch(t, carry):
+        load(t).start()
+        return carry
+
+    lax.fori_loop(0, SLOTS, prefetch, 0)
+
+    place = leaf_order(skel[...])
+    order_out[...] = place
+    places[zh, y, x] = place
+    pl.semaphore_wait(barrier, len(peers))
+
+    def share(src, slot, peer):
+        return pltpu.make_async_remote_copy(
+            src_ref=src,
+            dst_ref=src,
+            send_sem=place_send.at[slot],
+            recv_sem=place_recv.at[slot],
+            device_id=peer,
+            device_id_type=pl.DeviceIdType.MESH,
+        )
+
+    shared = []
+    for base, src, targets in (
+        (0, places.at[zh, y, x], peers[0:3]),
+        (3, places.at[zh, y], peers[3:6]),
+        (6, places.at[zh], peers[6:7]),
+    ):
+        stage = [share(src, base + k, peer) for k, peer in enumerate(targets)]
+        for copy in stage:
+            copy.start()
+        for copy in stage:
+            copy.wait_recv()
+        shared += stage
+
+    halves = []
+    rest = list(rest)
+    parts = []
+    for c, (_, rows) in enumerate(CHUNKS):
+        pair = []
+        for h in range(2):
+            part, o1, r1, l1, o2, r2, l2, zb = rest[:8]
+            rest = rest[8:]
+            first, second = (("x", x), ("y", y)) if h == 0 else (("y", y), ("x", x))
+            pair.append(
+                Half(
+                    part,
+                    ((o1, r1, l1), (o2, r2, l2)),
+                    zb,
+                    send.at[c, h],
+                    recv.at[c, h],
+                    rows,
+                    first,
+                    second,
+                    zh,
+                    dev,
+                )
+            )
+        halves.append(pair)
+
+    def multiply(t, carry):
+        xd, yd, zd = place_of(t)
+        dest = (zd * NY + yd) * NX + xd
+        slot = lax.rem(t, SLOTS)
+        load(t).wait()
+        rows_iota = lax.broadcasted_iota(jnp.int32, (LR, LR), 0).astype(F32)
+        pick = (rows_iota == places[zd, yd, xd]).astype(F32).astype(BF16)
+        for b in range(probes.shape[0] // LR):
+            cols = pl.ds(b * LR, LR)
+            moved = jnp.dot(pick, slots[slot, :, cols], preferred_element_type=F32)
+            own = leaf * (probes.shape[0] // LR) + b == grp * (NX * NY * NZ) + dest
+            permuted[:, cols] = jnp.where(own, 0.0, moved).astype(BF16)
+        for h in range(2):
+            product = jnp.dot(
+                permuted[...], probes[:, pl.ds(h * HALF, HALF)], preferred_element_type=F32
+            )
+            for c, (row, rows) in enumerate(CHUNKS):
+                at = (xd, yd, zd) if h == 0 else (yd, xd, zd)
+                halves[c][h].part[at] = product[row : row + rows]
+
+        @pl.when(t + SLOTS < NX * NY * NZ)
+        def _():
+            load(t + SLOTS).start()
+
+        return carry
+
+    a, b = halves
+    lax.fori_loop(0, 8, multiply, 0)
+    a[0].start(0, OPP_R, OPP_L)
+    lax.fori_loop(8, 14, multiply, 0)
+    a[1].start(0, OPP_R, OPP_L)
+    lax.fori_loop(14, 20, multiply, 0)
+    a[0].start(0, NEAR_RB)
+    lax.fori_loop(20, 26, multiply, 0)
+    a[0].start(0, NEAR_LA)
+    lax.fori_loop(26, 32, multiply, 0)
+    a[1].start(0, NEAR_RB, NEAR_LA)
+    for h in range(2):
+        a[h].relay(0)
+    for h in range(2):
+        b[h].start(0, OPP_R, OPP_L)
+    for h in range(2):
+        a[h].gather(0)
+        a[h].start(1, OPP_R, OPP_L, NEAR_RB, NEAR_LA)
+    for h in range(2):
+        b[h].start(0, NEAR_RB, NEAR_LA)
+    for h in range(2):
+        a[h].relay(1)
+    for h in range(2):
+        b[h].relay(0)
+    for h in range(2):
+        a[h].gather(1)
+        a[h].z_start()
+    for h in range(2):
+        out[pl.ds(0, 128), pl.ds(h * HALF, HALF)] = a[h].z_finish()
+    for h in range(2):
+        b[h].gather(0)
+        b[h].start(1, OPP_R, OPP_L, NEAR_RB, NEAR_LA)
+    for h in range(2):
+        b[h].relay(1)
+    for h in range(2):
+        b[h].gather(1)
+        b[h].z_start()
+    for h in range(2):
+        out[pl.ds(128, 128), pl.ds(h * HALF, HALF)] = b[h].z_finish()
+    for copy in shared:
+        copy.wait_send()
+    for pair in halves:
+        for half in pair:
+            for copy in half.started:
+                copy.wait_send()
+
+
+def reduced_rows(matrix, probes, skel):
+    depth = probes.shape[0]
+    scratch = [
+        pltpu.VMEM((SLOTS, LR, depth), BF16),
+        pltpu.VMEM((LR, depth), BF16),
+        pltpu.VMEM((NZ, NY, NX, 1, LR), F32),
+        pltpu.SemaphoreType.DMA((SLOTS,)),
+        pltpu.SemaphoreType.DMA((7,)),
+        pltpu.SemaphoreType.DMA((7,)),
+        pltpu.SemaphoreType.DMA((len(CHUNKS), 2, N_COPY)),
+        pltpu.SemaphoreType.DMA((len(CHUNKS), 2, N_COPY)),
+    ]
+    for _, rows in CHUNKS:
+        for _ in range(2):
+            scratch += [
+                pltpu.VMEM((4, 4, NZ, rows, HALF), F32),
+                pltpu.VMEM((2, 4, NZ, rows // 2, HALF), F32),
+                pltpu.VMEM((4, NZ, rows, HALF), F32),
+                pltpu.VMEM((4, NZ, rows, HALF), F32),
+                pltpu.VMEM((2, NZ, rows // 2, HALF), F32),
+                pltpu.VMEM((NZ, rows, HALF), F32),
+                pltpu.VMEM((NZ, rows, HALF), F32),
+                pltpu.VMEM((rows, HALF), F32),
+            ]
+    vmem = pl.BlockSpec(memory_space=pltpu.VMEM)
+    return pl.pallas_call(
+        kernel,
+        out_shape=(
+            jax.ShapeDtypeStruct((LR, probes.shape[1]), F32),
+            jax.ShapeDtypeStruct((1, LR), F32),
+        ),
+        in_specs=[pl.BlockSpec(memory_space=pl.ANY), vmem, vmem],
+        out_specs=(vmem, vmem),
+        scratch_shapes=scratch,
+        compiler_params=pltpu.CompilerParams(
+            collective_id=0, has_side_effects=True, vmem_limit_bytes=56 * 2**20
+        ),
+        name="reduced_rows",
+    )(matrix, probes, skel)
 
 
 def from_partner(value, axis, stride):
@@ -28,25 +402,14 @@
     grp_pos = lax.axis_index("grp")
     leaf_pos = lax.axis_index("leaf")
     device = grp_pos * n_leaf + leaf_pos
-    row_count, col_count = matrix.shape
-    leaf_rows = row_count // n_leaf
     rank = leaf_skeleton.shape[1]
     all_leaves = n_grp * n_leaf
     leaf_bits = n_leaf.bit_length() - 1
     grp_bits = n_grp.bit_length() - 1
     levels = leaf_bits + grp_bits
-    row_leaf = grp_pos * n_leaf + jnp.arange(row_count, dtype=jnp.int32) // leaf_rows
-    col_leaf = (leaf_pos * col_count + jnp.arange(col_count, dtype=jnp.int32)) // leaf_rows
-    block = jnp.where(
-        row_leaf[:, None] != col_leaf[None, :], matrix, jnp.zeros((), matrix.dtype)
-    )
-    samples_mine = lax.psum_scatter(
-        jnp.dot(block, probes, preferred_element_type=jnp.float32),
-        "leaf",
-        scatter_dimension=0,
-        tiled=True,
-    )
-    current = jnp.take(samples_mine, leaf_skeleton[0], axis=0)
+    moved, place = reduced_rows(matrix, probes, leaf_skeleton)
+    samples_mine = jnp.take(moved, place[0].astype(jnp.int32), axis=0)
+    current = moved[:rank]
     mine = jnp.zeros((2 * rank, samples_mine.shape[1]), jnp.float32)
     mine_picked = leaf_skeleton[0]
     offset = 0

time: 373 us -> 235 us (0.63)
  waiting for transfers between devices: 271 us -> 34.7 us
  Pallas kernels: 0 us -> 120 us
  matrix products: 19.8 us -> 2.98 us
  between operations: 14.5 us -> 0.98 us
  starting transfers between devices: 1.71 us -> 10.5 us
  local copies, waits for them, and re-layouts: 14.2 us -> 10.2 us
  other arithmetic: 51.2 us -> 55.1 us
    reduce_scatter x1 -> x0, waiting for transfers between devices: 228 us -> none  [on_device(): lax.psum_scatter(jnp.dot(block, probes, preferred_element_type=jnp.float3...]
    pallas_call x0 -> x1, Pallas kernels: none -> 120 us  [reduced_rows(): pl.pallas_call(kernel, out_shape=(jax.ShapeDtypeStruct((LR, probes.shape[...]
    dot_general x1 -> x0, matrix products: 15.8 us -> none  [on_device(): jnp.dot(block, probes, preferred_element_type=jnp.float32)]
    ppermute x7, waiting for transfers between devices: 43.6 us -> 34.7 us  [from_partner(): return lax.ppermute(value, axis, pairs)]
    ppermute x7, starting transfers between devices: 1.67 us -> 10.5 us  [from_partner(): return lax.ppermute(value, axis, pairs)]
    unnamed x20 -> x8, local copies, waits for them, and re-layouts: 4.81 us -> 0.73 us
  transfers between devices with their start and end apart: 8 -> 7, of which waited for: 8 -> 7; matrix products, arithmetic and copies ran while one was open for 0% -> 1% of each run, Pallas kernels for 0% -> 0%
where the time goes in v2:
time: 235 us; the launch traced here: 234 us
  Pallas kernels  120 us (51%)
  other arithmetic  55.1 us (23%)
  waiting for transfers between devices  34.7 us (15%)
  starting transfers between devices  10.5 us (4%)
  local copies, waits for them, and re-layouts  10.2 us (4%)
  matrix products  2.98 us (1%)
    pallas_call x1, Pallas kernels, reduced_rows(): pl.pallas_call(kernel, out_shape=(jax.ShapeDtypeStruct((LR, probes.shape[...  120 us
    ppermute x7, waiting for transfers between devices, from_partner(): return lax.ppermute(value, axis, pairs)  34.7 us
    another operation x4, other arithmetic, node_bases(): factor = jnp.linalg.cholesky(gram)  23.6 us
    another operation x3, other arithmetic, node_bases(): lax.linalg.triangular_solve(factor, first, left_side=True, lower=True, tr...  19.8 us
    ppermute x7, starting transfers between devices, from_partner(): return lax.ppermute(value, axis, pairs)  10.5 us
  transfers between devices with their start and end apart: 7, of which 7 were waited for; matrix products, arithmetic and copies ran while one was open for 1% of the time, Pallas kernels for 0%

profile of v2, /device:TPU:0, one launch (start us, length us, event | category | flops | bytes accessed | tf_op | source)
XLA Modules:
  0.0 234.0 jit_solution(14501499992629547572)
XLA Ops:
  0.6 119.6 %reduced_rows.1 = (f32[256,512]{1,0:T(8,128)}, f32[1,256]{1,0:T(1,128)}) custom-call(bf16[8192,1024]{1,0:T(8,128)(2,1)} %matrix.1, bf16[1024,512]{1,0:T(8,128)(2,1)} %probes.1, s32[1,128]{1,0:T(1,128)} %skel.1), custom_call_target="tpu_custom_call" | custom-call | tf_op jit(solution)/shard_map/reduced_rows/pallas_call | solution.py:365
  120.2 1.0 slice.23
  121.3 1.2 collective-permute-start
  122.5 0.8 compare_and_fusion
  123.3 4.5 %collective-permute-done = f32[128,512]{1,0:T(8,128)S(1)} collective-permute-done((f32[128,512]{1,0:T(8,128)S(1)}, f32[128,512]{1,0:T(8,128)S(1)}, u32[]{:S(2)}, u32[]{:S(2)}) %collective-permute-start) | collective-permute-done | bytes 262176 | tf_op jit(solution)/shard_map/ppermute | solution.py:384
  127.7 1.7 broadcast_select_fusion.7
  129.4 0.7 copy-done.1
  130.1 1.0 pad_maximum_fusion.1
  131.1 0.8 gather_fusion.2
  132.0 2.7 %collective-permute-start.1 = (f32[128,512]{1,0:T(8,128)S(1)}, f32[128,512]{1,0:T(8,128)S(1)}, u32[]{:S(2)}, u32[]{:S(2)}) collective-permute-start(f32[128,512]{1,0:T(8,128)S(1)} %broadcast_select_fusion.5), channel_id=1, source_target_pairs={{0,2},{1,3},{2,0},{3,1},{4,6},{5,7},{6,4},{7,5},{8,10},{9,11},{10,... | collective-permute-start | bytes 786440 | tf_op jit(solution)/shard_map/ppermute | solution.py:384
  134.7 5.2 %collective-permute-done.1 = f32[128,512]{1,0:T(8,128)S(1)} collective-permute-done((f32[128,512]{1,0:T(8,128)S(1)}, f32[128,512]{1,0:T(8,128)S(1)}, u32[]{:S(2)}, u32[]{:S(2)}) %collective-permute-start.1) | collective-permute-done | bytes 262176 | tf_op jit(solution)/shard_map/ppermute | solution.py:384
  139.9 0.1 broadcast_select_fusion.9
  140.1 0.8 gather_fusion.3
  140.9 1.1 collective-permute-start.2
  142.1 7.0 %collective-permute-done.2 = f32[128,512]{1,0:T(8,128)S(1)} collective-permute-done((f32[128,512]{1,0:T(8,128)S(1)}, f32[128,512]{1,0:T(8,128)S(1)}, u32[]{:S(2)}, u32[]{:S(2)}) %collective-permute-start.2) | collective-permute-done | bytes 262176 | tf_op jit(solution)/shard_map/ppermute | solution.py:384
  149.1 0.1 broadcast_select_fusion.11
  149.2 0.8 gather_fusion.4
  150.1 2.1 collective-permute-start.3
  152.2 0.6 compare_select_fusion.1
  152.9 5.2 %collective-permute-done.3 = f32[128,512]{1,0:T(8,128)S(1)} collective-permute-done((f32[128,512]{1,0:T(8,128)S(1)}, f32[128,512]{1,0:T(8,128)S(1)}, u32[]{:S(2)}, u32[]{:S(2)}) %collective-permute-start.3) | collective-permute-done | bytes 262176 | tf_op jit(solution)/shard_map/ppermute | solution.py:384
  158.0 0.1 broadcast_select_fusion.13
  158.2 0.8 gather_fusion.5
  159.0 2.2 collective-permute-start.4
  161.3 0.8 broadcast_select_fusion.24
  162.1 4.9 %collective-permute-done.4 = f32[128,512]{1,0:T(8,128)S(1)} collective-permute-done((f32[128,512]{1,0:T(8,128)S(1)}, f32[128,512]{1,0:T(8,128)S(1)}, u32[]{:S(2)}, u32[]{:S(2)}) %collective-permute-start.4) | collective-permute-done | bytes 262176 | tf_op jit(solution)/shard_map/ppermute | solution.py:384
  167.0 0.1 broadcast_select_fusion.15
  167.1 0.8 gather_fusion.6
  168.1 1.5 collective-permute-done.5
  169.6 0.9 broadcast_select_fusion.17
  170.5 1.1 pad_maximum_fusion.6
  171.6 0.8 gather_fusion.7
  172.4 0.8 broadcast_select_fusion
  173.2 1.0 collective-permute-start.6
  174.2 1.0 gather_fusion
  175.2 0.1 bitcast_select_fusion
  175.3 6.5 %collective-permute-done.6 = f32[128,512]{1,0:T(8,128)} collective-permute-done((f32[128,512]{1,0:T(8,128)}, f32[128,512]{1,0:T(8,128)}, u32[]{:S(2)}, u32[]{:S(2)}) %collective-permute-start.6) | collective-permute-done | bytes 262176 | tf_op jit(solution)/shard_map/ppermute | solution.py:384
  181.8 1.1 select_bitcast_fusion.1
  182.9 1.6 maximum_select_fusion
  184.5 0.1 pad_maximum_fusion
  184.6 2.1 gather_fusion.1
  186.7 0.8 fusion.2
  187.5 1.2 fusion
  188.9 23.5 %custom-call.9 = f32[2,128,128]{2,1,0:T(8,128)S(1)} custom-call(f32[2,128,128]{2,1,0:T(8,128)S(1)} %fusion.12), custom_call_target="Cholesky" | custom-call | tf_op jit(solution)/shard_map/jit(cholesky)/cholesky | solution.py:391
  212.4 0.1 compare_reduce_fusion
  212.6 19.7 %custom-call.10 = f32[2,1,128,128]{2,3,1,0:T(8,128)S(1)} custom-call(f32[2,1,128,128]{3,2,1,0:T(8,128)S(1)} %select_bitcast_fusion.2), custom_call_target="InvertDiagBlocksLowerTriangular" | custom-call | tf_op jit(solution)/shard_map/triangular_solve | solution.py:393
  232.3 0.6 fusion.10
  232.9 0.4 fusion.8
  233.3 0.7 fusion.18
  (34 shorter events, 1.0 us)
Async XLA Ops:
  0.6 160.6 %copy-start.2 = (s32[1,128]{1,0:T(1,128)S(1)}, s32[1,128]{1,0:T(1,128)}, u32[]{:S(2)}) copy-start(s32[1,128]{1,0:T(1,128)} %skel.1) | copy-start | bytes 1540
  120.2 47.9 %copy-start.3 = (f32[1,256]{1,0:T(1,128)S(1)}, f32[1,256]{1,0:T(1,128)}, u32[]{:S(2)}) copy-start(f32[1,256]{1,0:T(1,128)} %get-tuple-element.5) | copy-start | bytes 3076
  120.2 54.0 %copy-start = (f32[256,512]{1,0:T(8,128)S(1)}, f32[256,512]{1,0:T(8,128)}, u32[]{:S(2)}) copy-start(f32[256,512]{1,0:T(8,128)} %get-tuple-element.6) | copy-start | bytes 1572868
  121.3 6.5 %collective-permute-start = (f32[128,512]{1,0:T(8,128)S(1)}, f32[128,512]{1,0:T(8,128)S(1)}, u32[]{:S(2)}, u32[]{:S(2)}) collective-permute-start(f32[128,512]{1,0:T(8,128)S(1)} %slice.23), channel_id=1, source_target_pairs={{0,1},{1,0},{2,3},{3,2},{4,5},{5,4},{6,7},{7,6},{8,9},{9,8},{10,11... | collective-permute-start | bytes 786440 | tf_op jit(solution)/shard_map/ppermute | solution.py:384
  129.4 0.7 copy-start.1
  132.0 8.0 %collective-permute-start.1 = (f32[128,512]{1,0:T(8,128)S(1)}, f32[128,512]{1,0:T(8,128)S(1)}, u32[]{:S(2)}, u32[]{:S(2)}) collective-permute-start(f32[128,512]{1,0:T(8,128)S(1)} %broadcast_select_fusion.5), channel_id=1, source_target_pairs={{0,2},{1,3},{2,0},{3,1},{4,6},{5,7},{6,4},{7,5},{8,10},{9,11},{10,... | collective-permute-start | bytes 786440 | tf_op jit(solution)/shard_map/ppermute | solution.py:384
  140.9 8.1 %collective-permute-start.2 = (f32[128,512]{1,0:T(8,128)S(1)}, f32[128,512]{1,0:T(8,128)S(1)}, u32[]{:S(2)}, u32[]{:S(2)}) collective-permute-start(f32[128,512]{1,0:T(8,128)S(1)} %broadcast_select_fusion.4), channel_id=1, source_target_pairs={{0,4},{1,5},{2,6},{3,7},{4,0},{5,1},{6,2},{7,3},{8,12},{9,13},{10,... | collective-permute-start | bytes 786440 | tf_op jit(solution)/shard_map/ppermute | solution.py:384
  150.1 8.0 %collective-permute-start.3 = (f32[128,512]{1,0:T(8,128)S(1)}, f32[128,512]{1,0:T(8,128)S(1)}, u32[]{:S(2)}, u32[]{:S(2)}) collective-permute-start(f32[128,512]{1,0:T(8,128)S(1)} %broadcast_select_fusion.3), channel_id=1, source_target_pairs={{0,8},{1,9},{2,10},{3,11},{4,12},{5,13},{6,14},{7,15},{8,0},{9,1},... | collective-permute-start | bytes 786440 | tf_op jit(solution)/shard_map/ppermute | solution.py:384
  159.0 8.0 %collective-permute-start.4 = (f32[128,512]{1,0:T(8,128)S(1)}, f32[128,512]{1,0:T(8,128)S(1)}, u32[]{:S(2)}, u32[]{:S(2)}) collective-permute-start(f32[128,512]{1,0:T(8,128)S(1)} %broadcast_select_fusion.2), channel_id=1, source_target_pairs={{0,16},{1,17},{2,18},{3,19},{4,20},{5,21},{6,22},{7,23},{8,24},{9,... | collective-permute-start | bytes 786440 | tf_op jit(solution)/shard_map/ppermute | solution.py:384
  168.0 1.6 collective-permute-start.5
  173.2 8.7 %collective-permute-start.6 = (f32[128,512]{1,0:T(8,128)}, f32[128,512]{1,0:T(8,128)}, u32[]{:S(2)}, u32[]{:S(2)}) collective-permute-start(f32[128,512]{1,0:T(8,128)} %broadcast_select_fusion), channel_id=1, source_target_pairs={{0,64},{32,96},{64,0},{96,32},{1,65},{33,97},{65,1},{97,33},{2,66}... | collective-permute-start | bytes 786440 | tf_op jit(solution)/shard_map/ppermute | solution.py:384

commit v3 on v2

--- a/solution.py
+++ b/solution.py
@@ -11,6 +11,13 @@
 HALF = 256
 SLOTS = 8
 CHUNKS = ((0, 128), (128, 128))
+PIECES = 4
+PIECE = 128
+LEVELS = 7
+GROUP = NX * NY * NZ
+LEAVES = 128
+PANEL = 16
+HIGHEST = lax.Precision.HIGHEST
 F32 = jnp.float32
 BF16 = jnp.bfloat16
 ORDER = (
@@ -157,18 +164,74 @@
     return place[0:1]
 
 
+def selection(place):
+    return (lax.broadcasted_iota(jnp.int32, (LR, LR), 0).astype(F32) == place).astype(F32)
+
+
+def select(pick, value):
+    total = 0.0
+    for _ in range(3):
+        term = value.astype(BF16)
+        total = total + jnp.dot(pick, term, preferred_element_type=F32)
+        value = value - term.astype(F32)
+    return total
+
+
+def times_transposed(a, b):
+    return lax.dot_general(
+        a, b, (((1,), (1,)), ((), ())), precision=HIGHEST, preferred_element_type=F32
+    )
+
+
+def eliminate(panels):
+    lane = lax.broadcasted_iota(jnp.int32, panels[0].shape, 1)
+    sub = lax.broadcasted_iota(jnp.int32, panels[0].shape, 0)
+    for k in range(PANEL):
+        done = []
+        for p in panels:
+            row = jnp.where(lane[0:1] == k, 1.0, p[k : k + 1]) * (1.0 / p[k : k + 1, k : k + 1])
+            rest = jnp.where(lane == k, 0.0, p) - p[:, k : k + 1] * row
+            done.append(jnp.where(sub == k, row, rest))
+        panels = done
+    return panels
+
+
+def inverses(grams):
+    def body(_, grams):
+        panels = eliminate([g[:PANEL] for g in grams])
+        done = []
+        for g, p in zip(grams, panels):
+            rest = g[PANEL:]
+            lane = lax.broadcasted_iota(jnp.int32, rest.shape, 1)
+            rest = jnp.where(lane < PANEL, 0.0, rest) - jnp.dot(
+                rest[:, :PANEL], p, precision=HIGHEST, preferred_element_type=F32
+            )
+            done.append(pltpu.roll(jnp.concatenate([rest, p], 0), RANK - PANEL, 1))
+        return tuple(done)
+
+    return lax.fori_loop(0, RANK // PANEL, body, tuple(grams))
+
+
 def kernel(
     matrix,
     probes,
     skel,
-    out,
-    order_out,
+    node_skel,
+    leaf_out,
+    node_out,
     slots,
     permuted,
     places,
+    leaf_rows,
+    node_rows,
+    stack,
+    unpick,
+    weights,
     in_sem,
     place_send,
     place_recv,
+    tree_send,
+    tree_recv,
     send,
     recv,
     *rest,
@@ -189,6 +252,41 @@
     for peer in peers:
         pl.semaphore_signal(barrier, 1, device_id=peer, device_id_type=pl.DeviceIdType.MESH)
 
+    me = grp * GROUP + leaf
+    odd = lax.rem(me, 2) == 1
+    level = jnp.int32(1)
+    for k in range(1, LEVELS):
+        level = jnp.where(lax.rem(me, 2**k) == 0, k + 1, level)
+    step = sum(jnp.where(level == k, 2 ** (k - 1), 0) for k in range(1, LEVELS + 1))
+    node = sum(
+        jnp.where(level == k, LEAVES - (LEAVES >> (k - 1)) + me // 2**k, 0)
+        for k in range(1, LEVELS + 1)
+    )
+    side = lax.rem(me // (2 * step), 2)
+    parent = jnp.where(side == 0, me + step, me - step)
+    top = me == 0
+
+    def device_of(number):
+        number = lax.rem(number + LEAVES, LEAVES)
+        return {"grp": number // GROUP, "leaf": lax.rem(number, GROUP)}
+
+    def greet(number):
+        pl.semaphore_signal(
+            barrier, 1, device_id=device_of(number), device_id_type=pl.DeviceIdType.MESH
+        )
+
+    @pl.when(odd)
+    def _():
+        greet(me - 1)
+
+    @pl.when(jnp.logical_not(odd))
+    def _():
+        greet(jnp.where(top, LEAVES // 4, me - step // 2))
+        greet(jnp.where(top, 3 * LEAVES // 4, me + step // 2))
+
+    greeted = len(peers) + jnp.where(odd, 0, 1)
+    greeted = greeted + jnp.where(level < LEVELS, 1, 0) + jnp.where(level == LEVELS - 1, 1, 0)
+
     def place_of(t):
         pair = t // NZ
         i = sum(jnp.where(pair == k, o[0], 0) for k, o in enumerate(ORDER))
@@ -212,9 +310,10 @@
     lax.fori_loop(0, SLOTS, prefetch, 0)
 
     place = leaf_order(skel[...])
-    order_out[...] = place
     places[zh, y, x] = place
-    pl.semaphore_wait(barrier, len(peers))
+    node_pick = selection(leaf_order(node_skel[pl.ds(node, 1), :]))[:RANK].astype(BF16)
+    unpick[...] = selection(place).T
+    pl.semaphore_wait(barrier, greeted)
 
     def share(src, slot, peer):
         return pltpu.make_async_remote_copy(
@@ -313,12 +412,72 @@
     for h in range(2):
         a[h].relay(1)
     for h in range(2):
-        b[h].relay(0)
-    for h in range(2):
         a[h].gather(1)
         a[h].z_start()
     for h in range(2):
-        out[pl.ds(0, 128), pl.ds(h * HALF, HALF)] = a[h].z_finish()
+        b[h].relay(0)
+
+    def climb(src, c, slot, sem, to):
+        return pltpu.make_async_remote_copy(
+            src_ref=src.at[c],
+            dst_ref=stack.at[c, slot],
+            send_sem=tree_send.at[sem, c],
+            recv_sem=tree_recv.at[slot, c],
+            device_id=device_of(to),
+            device_id_type=pl.DeviceIdType.MESH,
+        )
+
+    for h in range(2):
+        rows = a[h].z_finish()
+        for c in range(2 * h, 2 * h + 2):
+            piece = rows[:, (c - 2 * h) * PIECE : (c - 2 * h + 1) * PIECE]
+            leaf_rows[c] = piece
+
+            @pl.when(odd)
+            def _():
+                stack[c, 1] = leaf_rows[c]
+
+            @pl.when(jnp.logical_not(odd))
+            def _():
+                climb(leaf_rows, c, 0, 0, me + 1).start()
+
+    sends = level < LEVELS
+    below_root = level == LEVELS - 1
+    for c in range(PIECES):
+        climb(leaf_rows, c, 0, 0, me + 1).wait_recv()
+
+        @pl.when(jnp.logical_not(odd))
+        def _():
+            climb(leaf_rows, c, 1, 0, me + 1).wait_recv()
+
+        node_rows[c] = select(node_pick, stack[c].reshape(LR, PIECE))
+
+        @pl.when(sends)
+        def _():
+            climb(node_rows, c, side, 1, parent).start()
+
+        @pl.when(below_root)
+        def _():
+            climb(node_rows, c, side, 2, 0).start()
+
+    grams = []
+    for rows in (leaf_rows, node_rows):
+        gram = 0.0
+        for c in range(PIECES):
+            gram = gram + times_transposed(rows[c], rows[c])
+        grams.append(gram)
+    leaf_inv, node_inv = inverses(grams)
+    known = 0.0
+    basis = 0.0
+    for c in range(PIECES):
+        weight = jnp.dot(leaf_inv, leaf_rows[c], precision=HIGHEST, preferred_element_type=F32)
+        weights[c] = weight
+        known = known + times_transposed(leaf_rows[c], weight)
+        weight = jnp.dot(node_inv, node_rows[c], precision=HIGHEST, preferred_element_type=F32)
+        basis = basis + times_transposed(stack[c].reshape(LR, PIECE), weight)
+    node_out[0] = basis
+    leaf_out[...] = select(unpick[:, :RANK].astype(BF16), known)
+
     for h in range(2):
         b[h].gather(0)
         b[h].start(1, OPP_R, OPP_L, NEAR_RB, NEAR_LA)
@@ -327,8 +486,29 @@
     for h in range(2):
         b[h].gather(1)
         b[h].z_start()
-    for h in range(2):
-        out[pl.ds(128, 128), pl.ds(h * HALF, HALF)] = b[h].z_finish()
+    basis = 0.0
+    for h in range(2):
+        rows = b[h].z_finish()
+        for c in range(2):
+            basis = basis + times_transposed(
+                rows[:, c * PIECE : (c + 1) * PIECE], weights[2 * h + c]
+            )
+    leaf_out[...] += select(unpick[:, RANK:].astype(BF16), basis)
+
+    for c in range(PIECES):
+
+        @pl.when(jnp.logical_not(odd))
+        def _():
+            climb(leaf_rows, c, 0, 0, me + 1).wait_send()
+
+        @pl.when(sends)
+        def _():
+            climb(node_rows, c, side, 1, parent).wait_send()
+
+        @pl.when(below_root)
+        def _():
+            climb(node_rows, c, side, 2, 0).wait_send()
+
     for copy in shared:
         copy.wait_send()
     for pair in halves:
@@ -337,15 +517,22 @@
                 copy.wait_send()
 
 
-def reduced_rows(matrix, probes, skel):
+def bases(matrix, probes, skel, node_skel):
     depth = probes.shape[0]
     scratch = [
         pltpu.VMEM((SLOTS, LR, depth), BF16),
         pltpu.VMEM((LR, depth), BF16),
         pltpu.VMEM((NZ, NY, NX, 1, LR), F32),
+        pltpu.VMEM((PIECES, RANK, PIECE), F32),
+        pltpu.VMEM((PIECES, RANK, PIECE), F32),
+        pltpu.VMEM((PIECES, 2, RANK, PIECE), F32),
+        pltpu.VMEM((LR, LR), F32),
+        pltpu.VMEM((PIECES, RANK, PIECE), F32),
         pltpu.SemaphoreType.DMA((SLOTS,)),
         pltpu.SemaphoreType.DMA((7,)),
         pltpu.SemaphoreType.DMA((7,)),
+        pltpu.SemaphoreType.DMA((3, PIECES)),
+        pltpu.SemaphoreType.DMA((2, PIECES)),
         pltpu.SemaphoreType.DMA((len(CHUNKS), 2, N_COPY)),
         pltpu.SemaphoreType.DMA((len(CHUNKS), 2, N_COPY)),
     ]
@@ -365,75 +552,21 @@
     return pl.pallas_call(
         kernel,
         out_shape=(
-            jax.ShapeDtypeStruct((LR, probes.shape[1]), F32),
-            jax.ShapeDtypeStruct((1, LR), F32),
+            jax.ShapeDtypeStruct((LR, RANK), F32),
+            jax.ShapeDtypeStruct((1, LR, RANK), F32),
         ),
-        in_specs=[pl.BlockSpec(memory_space=pl.ANY), vmem, vmem],
+        in_specs=[pl.BlockSpec(memory_space=pl.ANY), vmem, vmem, vmem],
         out_specs=(vmem, vmem),
         scratch_shapes=scratch,
         compiler_params=pltpu.CompilerParams(
             collective_id=0, has_side_effects=True, vmem_limit_bytes=56 * 2**20
         ),
-        name="reduced_rows",
-    )(matrix, probes, skel)
-
-
-def from_partner(value, axis, stride):
-    mask = 2**stride
-    pairs = [(source, source ^ mask) for source in range(lax.axis_size(axis))]
-    return lax.ppermute(value, axis, pairs)
-
-
-def node_bases(stacked, picked):
-    rows = jnp.take_along_axis(stacked, picked[:, :, None], axis=1)
-    gram = jnp.einsum("nks,nls->nkl", rows, rows, precision=lax.Precision.HIGHEST)
-    cross = jnp.einsum("nks,nis->nki", rows, stacked, precision=lax.Precision.HIGHEST)
-    factor = jnp.linalg.cholesky(gram)
-    first = lax.linalg.triangular_solve(factor, cross, left_side=True, lower=True)
-    solved = lax.linalg.triangular_solve(
-        factor, first, left_side=True, lower=True, transpose_a=True
-    )
-    return jnp.swapaxes(solved, 1, 2)
+        name="bases",
+    )(matrix, probes, skel, node_skel)
 
 
 def on_device(matrix, probes, leaf_skeleton, node_skeleton):
-    n_grp = lax.axis_size("grp")
-    n_leaf = lax.axis_size("leaf")
-    grp_pos = lax.axis_index("grp")
-    leaf_pos = lax.axis_index("leaf")
-    device = grp_pos * n_leaf + leaf_pos
-    rank = leaf_skeleton.shape[1]
-    all_leaves = n_grp * n_leaf
-    leaf_bits = n_leaf.bit_length() - 1
-    grp_bits = n_grp.bit_length() - 1
-    levels = leaf_bits + grp_bits
-    moved, place = reduced_rows(matrix, probes, leaf_skeleton)
-    samples_mine = jnp.take(moved, place[0].astype(jnp.int32), axis=0)
-    current = moved[:rank]
-    mine = jnp.zeros((2 * rank, samples_mine.shape[1]), jnp.float32)
-    mine_picked = leaf_skeleton[0]
-    offset = 0
-    for level in range(1, levels + 1):
-        if level <= leaf_bits:
-            bit = leaf_pos >> (level - 1) & 1
-            partner = from_partner(current, "leaf", level - 1)
-        else:
-            bit = grp_pos >> (level - 1 - leaf_bits) & 1
-            partner = from_partner(current, "grp", level - 1 - leaf_bits)
-        lower = jnp.where(bit == 1, partner, current)
-        upper = jnp.where(bit == 1, current, partner)
-        stacked = jnp.concatenate([lower, upper], axis=0)
-        picked = node_skeleton[offset + (device >> level)]
-        offset += all_leaves >> level
-        select = (device % (1 << level) == 1 << level - 1) | (device == 0) & (level == levels)
-        mine = jnp.where(select, stacked, mine)
-        mine_picked = jnp.where(select, picked, mine_picked)
-        if level < levels:
-            current = jnp.take(stacked, picked, axis=0)
-    bases = node_bases(
-        jnp.stack([samples_mine, mine]), jnp.stack([leaf_skeleton[0], mine_picked])
-    )
-    return (bases[0], bases[1:])
+    return bases(matrix, probes, leaf_skeleton, node_skeleton)
 
 
 def solution(mesh):

time: 235 us -> 169 us (0.72)
  other arithmetic: 55.1 us -> 0 us
  Pallas kernels: 120 us -> 164 us
  waiting for transfers between devices: 34.7 us -> 0 us
  starting transfers between devices: 10.5 us -> 0 us
  local copies, waits for them, and re-layouts: 10.2 us -> 3.14 us
  matrix products: 2.98 us -> 0 us
    pallas_call x1, Pallas kernels: 120 us -> 164 us  [bases(): pl.pallas_call(kernel, out_shape=(jax.ShapeDtypeStruct((LR, RANK), F32),...]
    another operation x8 -> x0, other arithmetic: 43.5 us -> none  [the longest x4 23.6 us: node_bases(): factor = jnp.linalg.cholesky(gram)]
    ppermute x7 -> x0, waiting for transfers between devices: 34.7 us -> none  [from_partner(): return lax.ppermute(value, axis, pairs)]
    ppermute x7 -> x0, starting transfers between devices: 10.5 us -> none  [from_partner(): return lax.ppermute(value, axis, pairs)]
    gather x8 -> x0, local copies, waits for them, and re-layouts: 7.61 us -> none  [the longest x6 4.54 us: on_device(): current = jnp.take(stacked, picked, axis=0)]
    select_n x16 -> x0, other arithmetic: 7.48 us -> none  [the longest x6 3.04 us: on_device(): lower = jnp.where(bit == 1, partner, current)]
    concatenate x7 -> x0, other arithmetic: 3.24 us -> none  [on_device(): stacked = jnp.concatenate([lower, upper], axis=0)]
    unnamed x8 -> x2, local copies, waits for them, and re-layouts: 0.73 us -> 3.14 us
  transfers between devices with their start and end apart: 7 -> 0, of which waited for: 7 -> 0; matrix products, arithmetic and copies ran while one was open for 1% -> 0% of each run, Pallas kernels for 0% -> 0%
where the time goes in v3:
time: 169 us; the launch traced here: 168 us
  Pallas kernels  164 us (97%)
  local copies, waits for them, and re-layouts  3.14 us (2%)
    pallas_call x1, Pallas kernels, bases(): pl.pallas_call(kernel, out_shape=(jax.ShapeDtypeStruct((LR, RANK), F32),...  164 us

profile of v3, /device:TPU:0, one launch (start us, length us, event | category | flops | bytes accessed | tf_op | source)
XLA Modules:
  0.0 168.1 jit_solution(2759526105152803999)
XLA Ops:
  0.6 164.3 %bases.1 = (f32[256,128]{1,0:T(8,128)}, f32[1,256,128]{2,1,0:T(8,128)}) custom-call(bf16[8192,1024]{1,0:T(8,128)(2,1)} %matrix.1, bf16[1024,512]{1,0:T(8,128)(2,1)} %probes.1, s32[1,128]{1,0:T(1,128)} %skel.1, s32[127,128]{1,0:T(8,128)} %node_skel.1), custom_call_target="tpu_custom_call" | custom-call | tf_op jit(solution)/shard_map/bases/pallas_call | solution.py:552
  164.9 1.6 copy.8
  166.5 1.6 copy.9

commit v4 on v3

--- a/solution.py
+++ b/solution.py
@@ -10,7 +10,7 @@
 RANK = 128
 HALF = 256
 SLOTS = 8
-CHUNKS = ((0, 128), (128, 128))
+CHUNKS = ((0, 128, False), (128, 64, False), (192, 64, True))
 PIECES = 4
 PIECE = 128
 LEVELS = 7
@@ -30,7 +30,7 @@
 OPP_R, OPP_L, NEAR_RA, NEAR_RB, NEAR_LA, NEAR_LB = range(6)
 PASS = 6
 Z_COPY = 2 * PASS
-N_COPY = 2 * PASS + 1
+N_COPY = 2 * PASS + 4
 
 
 def mod4(v):
@@ -38,10 +38,12 @@
 
 
 class Half:
-    def __init__(self, part, bufs, zbuf, send, recv, rows, first, second, zh, dev):
-        self.part, self.bufs, self.zbuf = part, bufs, zbuf
+    def __init__(self, part, bufs, zbuf, send, recv, rows, z_first, first, second, zh, dev):
+        self.whole, self.bufs, self.zbuf = part, bufs, zbuf
+        self.part = part.at[zh] if z_first else part
         self.send, self.recv = send, recv
         self.rows = rows
+        self.z_first = z_first
         self.axes = (first, second)
         self.zh = zh
         self.dev = dev
@@ -51,13 +53,30 @@
         if phase == 0:
             return self.part.at[index]
         return self.part.at[self.axes[0][1], index]
+
+    def lead(self, phase):
+        return 2 - phase - self.z_first
+
+    def begin(self, copy):
+        copy.start()
+        self.started.append(copy)
+
+    def remote(self, src, dst, slot, to):
+        return pltpu.make_async_remote_copy(
+            src_ref=src,
+            dst_ref=dst,
+            send_sem=self.send.at[slot],
+            recv_sem=self.recv.at[slot],
+            device_id=to,
+            device_id_type=pl.DeviceIdType.MESH,
+        )
 
     def copy(self, phase, kind):
         name, me = self.axes[phase]
         half = self.rows // 2
         opp, near_r, near_l = self.bufs[phase]
         lo, hi = pl.ds(0, half), pl.ds(half, half)
-        lead = (slice(None),) * (2 if phase == 0 else 1)
+        lead = (slice(None),) * self.lead(phase)
         right, left = mod4(me + 1), mod4(me - 1)
         index, rows, dst, to = {
             OPP_R: (mod4(me + 2), lo, opp.at[0], right),
@@ -67,21 +86,16 @@
             NEAR_LA: (left, lo, near_l.at[(*lead, lo)], left),
             NEAR_LB: (left, hi, near_l.at[(*lead, hi)], left),
         }[kind]
-        slot = phase * PASS + kind
-        return pltpu.make_async_remote_copy(
-            src_ref=self.block(phase, index).at[(*lead, rows)],
-            dst_ref=dst,
-            send_sem=self.send.at[slot],
-            recv_sem=self.recv.at[slot],
-            device_id=self.dev(**{name: to}),
-            device_id_type=pl.DeviceIdType.MESH,
+        return self.remote(
+            self.block(phase, index).at[(*lead, rows)],
+            dst,
+            phase * PASS + kind,
+            self.dev(**{name: to}),
         )
 
     def start(self, phase, *kinds):
         for kind in kinds:
-            copy = self.copy(phase, kind)
-            copy.start()
-            self.started.append(copy)
+            self.begin(self.copy(phase, kind))
 
     def wait(self, phase, kind):
         self.copy(phase, kind).wait_recv()
@@ -95,54 +109,62 @@
             (OPP_L, 1, mod4(me - 1), half, NEAR_LB),
         ):
             self.wait(phase, kind)
-            self.add(phase, index, row, half, (opp.at[side],), 0)
+            self.add(self.block(phase, index), phase, row, half, (opp.at[side],))
             self.start(phase, on)
 
     def gather(self, phase):
         me = self.axes[phase][1]
         for kind in (NEAR_RB, NEAR_LA, NEAR_RA, NEAR_LB):
             self.wait(phase, kind)
-        self.add(phase, me, 0, self.rows, self.bufs[phase][1:], 0)
-
-    def add(self, phase, index, row, count, terms, term_row):
-        target = self.block(phase, index)
-        rows, term_rows = pl.ds(row, count), pl.ds(term_row, count)
-        if phase == 0:
-
-            def step(i, carry):
-                at = (i // NZ, lax.rem(i, NZ))
-                value = target[(*at, rows)]
-                for term in terms:
-                    value = value + term[(*at, term_rows)]
-                target[(*at, rows)] = value
-                return carry
-
-            lax.fori_loop(0, 4 * NZ, step, 0)
+        self.add(self.block(phase, me), phase, 0, self.rows, self.bufs[phase][1:])
+
+    def add(self, target, phase, row, count, terms):
+        rows, term_rows = pl.ds(row, count), pl.ds(0, count)
+
+        def step(at):
+            value = target[(*at, rows)]
+            for term in terms:
+                value = value + term[(*at, term_rows)]
+            target[(*at, rows)] = value
+
+        if self.lead(phase) == 0:
+            step(())
+        elif self.lead(phase) == 1:
+            lax.fori_loop(0, NZ if phase else 4, lambda i, c: (step((i,)), c)[1], 0)
         else:
-            for z in range(NZ):
-                value = target[z, rows]
-                for term in terms:
-                    value = value + term[z, term_rows]
-                target[z, rows] = value
-
-    def z_copy(self):
-        return pltpu.make_async_remote_copy(
-            src_ref=self.part.at[self.axes[0][1], self.axes[1][1], 1 - self.zh],
-            dst_ref=self.zbuf,
-            send_sem=self.send.at[Z_COPY],
-            recv_sem=self.recv.at[Z_COPY],
-            device_id=self.dev(z=1 - self.zh),
-            device_id_type=pl.DeviceIdType.MESH,
-        )
-
-    def z_start(self):
-        copy = self.z_copy()
-        copy.start()
-        self.started.append(copy)
-
-    def z_finish(self):
+            lax.fori_loop(0, 4 * NZ, lambda i, c: (step((i // NZ, lax.rem(i, NZ))), c)[1], 0)
+
+    def z_copy(self, x=None):
+        to = self.dev(z=1 - self.zh)
+        if not self.z_first:
+            src = self.part.at[self.axes[0][1], self.axes[1][1], 1 - self.zh]
+            return self.remote(src, self.zbuf, 2 * PASS, to)
+        steps, x = x
+        at = (x,) if self.axes[0][0] == "x" else (slice(None), x)
+        return self.remote(
+            self.whole.at[(1 - self.zh, *at)], self.zbuf.at[at], 2 * PASS + steps, to
+        )
+
+    def z_start(self, x=None):
+        self.begin(self.z_copy(x))
+
+    def z_merge(self, xs):
+        for x in xs:
+            self.z_copy(x).wait_recv()
+
+        def step(i, carry):
+            at = (i // 4, lax.rem(i, 4))
+            self.part[at] += self.zbuf[at]
+            return carry
+
+        lax.fori_loop(0, 16, step, 0)
+
+    def finish(self):
+        at = (self.axes[0][1], self.axes[1][1])
+        if self.z_first:
+            return self.part[at]
         self.z_copy().wait_recv()
-        return self.part[self.axes[0][1], self.axes[1][1], self.zh] + self.zbuf[...]
+        return self.part[(*at, self.zh)] + self.zbuf[...]
 
 
 def leaf_order(skel):
@@ -246,11 +268,15 @@
         return {"leaf": (z * NY + y) * NX + x}
 
     barrier = pltpu.get_barrier_semaphore()
-    peers = [dev(x=mod4(x + k)) for k in (1, 2, 3)]
-    peers += [dev(y=mod4(y + k)) for k in (1, 2, 3)]
-    peers += [dev(z=1 - zh)]
-    for peer in peers:
-        pl.semaphore_signal(barrier, 1, device_id=peer, device_id_type=pl.DeviceIdType.MESH)
+
+    def peer(k):
+        return {"leaf": lax.rem(leaf + k, GROUP)}
+
+    def greet_peer(k, carry):
+        pl.semaphore_signal(barrier, 1, device_id=peer(k), device_id_type=pl.DeviceIdType.MESH)
+        return carry
+
+    lax.fori_loop(1, GROUP, greet_peer, 0)
 
     me = grp * GROUP + leaf
     odd = lax.rem(me, 2) == 1
@@ -284,7 +310,7 @@
         greet(jnp.where(top, LEAVES // 4, me - step // 2))
         greet(jnp.where(top, 3 * LEAVES // 4, me + step // 2))
 
-    greeted = len(peers) + jnp.where(odd, 0, 1)
+    greeted = GROUP - 1 + jnp.where(odd, 0, 1)
     greeted = greeted + jnp.where(level < LEVELS, 1, 0) + jnp.where(level == LEVELS - 1, 1, 0)
 
     def place_of(t):
@@ -310,38 +336,40 @@
     lax.fori_loop(0, SLOTS, prefetch, 0)
 
     place = leaf_order(skel[...])
-    places[zh, y, x] = place
+    places[leaf] = place
+    pl.semaphore_wait(barrier, greeted)
+
+    def share(k):
+        return pltpu.make_async_remote_copy(
+            src_ref=places.at[leaf],
+            dst_ref=places.at[leaf],
+            send_sem=place_send.at[k - 1],
+            recv_sem=place_recv.at[k - 1],
+            device_id=peer(k),
+            device_id_type=pl.DeviceIdType.MESH,
+        )
+
+    def share_start(k, carry):
+        share(k).start()
+        return carry
+
+    def share_arrived(k, carry):
+        share(k).wait_recv()
+        return carry
+
+    def share_sent(k, carry):
+        share(k).wait_send()
+        return carry
+
+    lax.fori_loop(1, GROUP, share_start, 0)
     node_pick = selection(leaf_order(node_skel[pl.ds(node, 1), :]))[:RANK].astype(BF16)
     unpick[...] = selection(place).T
-    pl.semaphore_wait(barrier, greeted)
-
-    def share(src, slot, peer):
-        return pltpu.make_async_remote_copy(
-            src_ref=src,
-            dst_ref=src,
-            send_sem=place_send.at[slot],
-            recv_sem=place_recv.at[slot],
-            device_id=peer,
-            device_id_type=pl.DeviceIdType.MESH,
-        )
-
-    shared = []
-    for base, src, targets in (
-        (0, places.at[zh, y, x], peers[0:3]),
-        (3, places.at[zh, y], peers[3:6]),
-        (6, places.at[zh], peers[6:7]),
-    ):
-        stage = [share(src, base + k, peer) for k, peer in enumerate(targets)]
-        for copy in stage:
-            copy.start()
-        for copy in stage:
-            copy.wait_recv()
-        shared += stage
+    lax.fori_loop(1, GROUP, share_arrived, 0)
 
     halves = []
     rest = list(rest)
     parts = []
-    for c, (_, rows) in enumerate(CHUNKS):
+    for c, (_, rows, z_first) in enumerate(CHUNKS):
         pair = []
         for h in range(2):
             part, o1, r1, l1, o2, r2, l2, zb = rest[:8]
@@ -355,6 +383,7 @@
                     send.at[c, h],
                     recv.at[c, h],
                     rows,
+                    z_first,
                     first,
                     second,
                     zh,
@@ -369,7 +398,7 @@
         slot = lax.rem(t, SLOTS)
         load(t).wait()
         rows_iota = lax.broadcasted_iota(jnp.int32, (LR, LR), 0).astype(F32)
-        pick = (rows_iota == places[zd, yd, xd]).astype(F32).astype(BF16)
+        pick = (rows_iota == places[dest]).astype(F32).astype(BF16)
         for b in range(probes.shape[0] // LR):
             cols = pl.ds(b * LR, LR)
             moved = jnp.dot(pick, slots[slot, :, cols], preferred_element_type=F32)
@@ -379,9 +408,10 @@
             product = jnp.dot(
                 permuted[...], probes[:, pl.ds(h * HALF, HALF)], preferred_element_type=F32
             )
-            for c, (row, rows) in enumerate(CHUNKS):
-                at = (xd, yd, zd) if h == 0 else (yd, xd, zd)
-                halves[c][h].part[at] = product[row : row + rows]
+            for c, (row, rows, z_first) in enumerate(CHUNKS):
+                at = (xd, yd) if h == 0 else (yd, xd)
+                at = (zd, *at) if z_first else (*at, zd)
+                halves[c][h].whole[at] = product[row : row + rows]
 
         @pl.when(t + SLOTS < NX * NY * NZ)
         def _():
@@ -389,28 +419,37 @@
 
         return carry
 
-    a, b = halves
+    a, b, d = halves
+    xs = [(k, mod4(x + k)) for k in range(4)]
     lax.fori_loop(0, 8, multiply, 0)
     a[0].start(0, OPP_R, OPP_L)
+    for h in range(2):
+        d[h].z_start(xs[2])
     lax.fori_loop(8, 14, multiply, 0)
     a[1].start(0, OPP_R, OPP_L)
     lax.fori_loop(14, 20, multiply, 0)
     a[0].start(0, NEAR_RB)
+    for h in range(2):
+        d[h].z_start(xs[1])
     lax.fori_loop(20, 26, multiply, 0)
     a[0].start(0, NEAR_LA)
+    for h in range(2):
+        d[h].z_start(xs[3])
     lax.fori_loop(26, 32, multiply, 0)
     a[1].start(0, NEAR_RB, NEAR_LA)
     for h in range(2):
+        d[h].z_start(xs[0])
+    for h in range(2):
         a[h].relay(0)
-    for h in range(2):
-        b[h].start(0, OPP_R, OPP_L)
     for h in range(2):
         a[h].gather(0)
         a[h].start(1, OPP_R, OPP_L, NEAR_RB, NEAR_LA)
     for h in range(2):
+        b[h].start(0, OPP_R, OPP_L)
+    for h in range(2):
+        a[h].relay(1)
+    for h in range(2):
         b[h].start(0, NEAR_RB, NEAR_LA)
-    for h in range(2):
-        a[h].relay(1)
     for h in range(2):
         a[h].gather(1)
         a[h].z_start()
@@ -428,7 +467,7 @@
         )
 
     for h in range(2):
-        rows = a[h].z_finish()
+        rows = a[h].finish()
         for c in range(2 * h, 2 * h + 2):
             piece = rows[:, (c - 2 * h) * PIECE : (c - 2 * h + 1) * PIECE]
             leaf_rows[c] = piece
@@ -443,30 +482,58 @@
 
     sends = level < LEVELS
     below_root = level == LEVELS - 1
-    for c in range(PIECES):
-        climb(leaf_rows, c, 0, 0, me + 1).wait_recv()
-
-        @pl.when(jnp.logical_not(odd))
+
+    def tree(low, high):
+        @pl.when(jnp.logical_and(level >= low, level <= high))
         def _():
-            climb(leaf_rows, c, 1, 0, me + 1).wait_recv()
-
-        node_rows[c] = select(node_pick, stack[c].reshape(LR, PIECE))
-
-        @pl.when(sends)
-        def _():
-            climb(node_rows, c, side, 1, parent).start()
-
-        @pl.when(below_root)
-        def _():
-            climb(node_rows, c, side, 2, 0).start()
-
-    grams = []
-    for rows in (leaf_rows, node_rows):
+            for c in range(PIECES):
+                climb(leaf_rows, c, 0, 0, me + 1).wait_recv()
+
+                @pl.when(jnp.logical_not(odd))
+                def _():
+                    climb(leaf_rows, c, 1, 0, me + 1).wait_recv()
+
+                node_rows[c] = select(node_pick, stack[c].reshape(LR, PIECE))
+
+                @pl.when(sends)
+                def _():
+                    climb(node_rows, c, side, 1, parent).start()
+
+                @pl.when(below_root)
+                def _():
+                    climb(node_rows, c, side, 2, 0).start()
+
+    def gram_of(rows):
         gram = 0.0
         for c in range(PIECES):
             gram = gram + times_transposed(rows[c], rows[c])
-        grams.append(gram)
-    leaf_inv, node_inv = inverses(grams)
+        return gram
+
+    tree(1, 2)
+    for h in range(2):
+        b[h].gather(0)
+        b[h].start(1, OPP_R, OPP_L, NEAR_RB, NEAR_LA)
+    tree(3, 3)
+    for h in range(2):
+        b[h].relay(1)
+    tree(4, 4)
+    for h in range(2):
+        d[h].z_merge(xs)
+        d[h].start(0, OPP_R, OPP_L, NEAR_RB, NEAR_LA)
+    tree(5, 5)
+    for h in range(2):
+        b[h].gather(1)
+        b[h].z_start()
+    for h in range(2):
+        d[h].relay(0)
+    tree(6, 6)
+    for h in range(2):
+        d[h].gather(0)
+        d[h].start(1, OPP_R, OPP_L, NEAR_RB, NEAR_LA)
+    tree(7, 7)
+    for h in range(2):
+        d[h].relay(1)
+    leaf_inv, node_inv = inverses((gram_of(leaf_rows), gram_of(node_rows)))
     known = 0.0
     basis = 0.0
     for c in range(PIECES):
@@ -478,22 +545,19 @@
     node_out[0] = basis
     leaf_out[...] = select(unpick[:, :RANK].astype(BF16), known)
 
-    for h in range(2):
-        b[h].gather(0)
-        b[h].start(1, OPP_R, OPP_L, NEAR_RB, NEAR_LA)
-    for h in range(2):
-        b[h].relay(1)
-    for h in range(2):
-        b[h].gather(1)
-        b[h].z_start()
-    basis = 0.0
-    for h in range(2):
-        rows = b[h].z_finish()
-        for c in range(2):
-            basis = basis + times_transposed(
-                rows[:, c * PIECE : (c + 1) * PIECE], weights[2 * h + c]
-            )
-    leaf_out[...] += select(unpick[:, RANK:].astype(BF16), basis)
+    found = []
+    for part in (b, d):
+        basis = 0.0
+        for h in range(2):
+            if part is d:
+                part[h].gather(1)
+            rows = part[h].finish()
+            for c in range(2):
+                basis = basis + times_transposed(
+                    rows[:, c * PIECE : (c + 1) * PIECE], weights[2 * h + c]
+                )
+        found.append(basis)
+    leaf_out[...] += select(unpick[:, RANK:].astype(BF16), jnp.concatenate(found, 0))
 
     for c in range(PIECES):
 
@@ -509,8 +573,7 @@
         def _():
             climb(node_rows, c, side, 2, 0).wait_send()
 
-    for copy in shared:
-        copy.wait_send()
+    lax.fori_loop(1, GROUP, share_sent, 0)
     for pair in halves:
         for half in pair:
             for copy in half.started:
@@ -522,31 +585,32 @@
     scratch = [
         pltpu.VMEM((SLOTS, LR, depth), BF16),
         pltpu.VMEM((LR, depth), BF16),
-        pltpu.VMEM((NZ, NY, NX, 1, LR), F32),
+        pltpu.VMEM((GROUP, 1, LR), F32),
         pltpu.VMEM((PIECES, RANK, PIECE), F32),
         pltpu.VMEM((PIECES, RANK, PIECE), F32),
         pltpu.VMEM((PIECES, 2, RANK, PIECE), F32),
         pltpu.VMEM((LR, LR), F32),
         pltpu.VMEM((PIECES, RANK, PIECE), F32),
         pltpu.SemaphoreType.DMA((SLOTS,)),
-        pltpu.SemaphoreType.DMA((7,)),
-        pltpu.SemaphoreType.DMA((7,)),
+        pltpu.SemaphoreType.DMA((GROUP - 1,)),
+        pltpu.SemaphoreType.DMA((GROUP - 1,)),
         pltpu.SemaphoreType.DMA((3, PIECES)),
         pltpu.SemaphoreType.DMA((2, PIECES)),
         pltpu.SemaphoreType.DMA((len(CHUNKS), 2, N_COPY)),
         pltpu.SemaphoreType.DMA((len(CHUNKS), 2, N_COPY)),
     ]
-    for _, rows in CHUNKS:
+    for _, rows, z_first in CHUNKS:
+        z = () if z_first else (NZ,)
         for _ in range(2):
             scratch += [
-                pltpu.VMEM((4, 4, NZ, rows, HALF), F32),
-                pltpu.VMEM((2, 4, NZ, rows // 2, HALF), F32),
-                pltpu.VMEM((4, NZ, rows, HALF), F32),
-                pltpu.VMEM((4, NZ, rows, HALF), F32),
-                pltpu.VMEM((2, NZ, rows // 2, HALF), F32),
-                pltpu.VMEM((NZ, rows, HALF), F32),
-                pltpu.VMEM((NZ, rows, HALF), F32),
-                pltpu.VMEM((rows, HALF), F32),
+                pltpu.VMEM((NZ, 4, 4, rows, HALF) if z_first else (4, 4, NZ, rows, HALF), F32),
+                pltpu.VMEM((2, 4, *z, rows // 2, HALF), F32),
+                pltpu.VMEM((4, *z, rows, HALF), F32),
+                pltpu.VMEM((4, *z, rows, HALF), F32),
+                pltpu.VMEM((2, *z, rows // 2, HALF), F32),
+                pltpu.VMEM((*z, rows, HALF), F32),
+                pltpu.VMEM((*z, rows, HALF), F32),
+                pltpu.VMEM((4, 4, rows, HALF) if z_first else (rows, HALF), F32),
             ]
     vmem = pl.BlockSpec(memory_space=pltpu.VMEM)
     return pl.pallas_call(

time: 169 us -> 145 us (0.86)
  Pallas kernels: 164 us -> 142 us
    pallas_call x1, Pallas kernels: 164 us -> 142 us  [bases(): pl.pallas_call(kernel, out_shape=(jax.ShapeDtypeStruct((LR, RANK), F32),...]
where the time goes in v4:
time: 145 us
  Pallas kernels  142 us (98%)
  local copies, waits for them, and re-layouts  3.14 us (2%)
    pallas_call x1, Pallas kernels, bases(): pl.pallas_call(kernel, out_shape=(jax.ShapeDtypeStruct((LR, RANK), F32),...  142 us
    unnamed x2, local copies, waits for them, and re-layouts  3.14 us

profile of v4, /device:TPU:0, one launch (start us, length us, event | category | flops | bytes accessed | tf_op | source)
XLA Modules:
  0.0 145.3 jit_solution(14271869291642209590)
XLA Ops:
  0.6 141.6 %bases.1 = (f32[256,128]{1,0:T(8,128)}, f32[1,256,128]{2,1,0:T(8,128)}) custom-call(bf16[8192,1024]{1,0:T(8,128)(2,1)} %matrix.1, bf16[1024,512]{1,0:T(8,128)(2,1)} %probes.1, s32[1,128]{1,0:T(1,128)} %skel.1, s32[127,128]{1,0:T(8,128)} %node_skel.1), custom_call_target="tpu_custom_call" | custom-call | tf_op jit(solution)/shard_map/bases/pallas_call | solution.py:616
  142.2 1.6 %copy.8 = f32[256,128]{1,0:T(8,128)} copy(f32[256,128]{1,0:T(8,128)} %get-tuple-element.4) | data formatting | bytes 262144
  143.8 1.6 %copy.9 = f32[1,256,128]{2,1,0:T(8,128)} copy(f32[1,256,128]{2,1,0:T(8,128)} %get-tuple-element.5) | data formatting | bytes 262144

commit v5 on v4

--- a/solution.py
+++ b/solution.py
@@ -10,13 +10,14 @@
 RANK = 128
 HALF = 256
 SLOTS = 8
-CHUNKS = ((0, 128, False), (128, 64, False), (192, 64, True))
+CHUNKS = ((0, 64, False), (64, 64, False), (128, 64, False), (192, 64, True))
 PIECES = 4
 PIECE = 128
 LEVELS = 7
 GROUP = NX * NY * NZ
 LEAVES = 128
 PANEL = 16
+AHEAD = 8
 HIGHEST = lax.Precision.HIGHEST
 F32 = jnp.float32
 BF16 = jnp.bfloat16
@@ -206,15 +207,26 @@
 
 
 def eliminate(panels):
+    panels = list(panels)
     lane = lax.broadcasted_iota(jnp.int32, panels[0].shape, 1)
     sub = lax.broadcasted_iota(jnp.int32, panels[0].shape, 0)
-    for k in range(PANEL):
-        done = []
-        for p in panels:
-            row = jnp.where(lane[0:1] == k, 1.0, p[k : k + 1]) * (1.0 / p[k : k + 1, k : k + 1])
-            rest = jnp.where(lane == k, 0.0, p) - p[:, k : k + 1] * row
-            done.append(jnp.where(sub == k, row, rest))
-        panels = done
+    for base in range(0, PANEL, AHEAD):
+        columns = [
+            [jnp.broadcast_to(p[:, k : k + 1], p.shape) for k in range(base, base + AHEAD)]
+            for p in panels
+        ]
+        for ahead in range(AHEAD):
+            k = base + ahead
+            for n, p in enumerate(panels):
+                column = columns[n][ahead]
+                scale = 1.0 / column[k : k + 1]
+                row = jnp.where(lane[0:1] == k, 1.0, p[k : k + 1]) * scale
+                rest = jnp.where(lane == k, 0.0, p) - column * row
+                panels[n] = jnp.where(sub == k, row, rest)
+                for later in range(ahead + 1, AHEAD):
+                    other = columns[n][later]
+                    row = other[k : k + 1] * scale
+                    columns[n][later] = jnp.where(sub == k, row, other - column * row)
     return panels
 
 
@@ -313,10 +325,13 @@
     greeted = GROUP - 1 + jnp.where(odd, 0, 1)
     greeted = greeted + jnp.where(level < LEVELS, 1, 0) + jnp.where(level == LEVELS - 1, 1, 0)
 
-    def place_of(t):
-        pair = t // NZ
+    def steps_of(pair):
         i = sum(jnp.where(pair == k, o[0], 0) for k, o in enumerate(ORDER))
         j = sum(jnp.where(pair == k, o[1], 0) for k, o in enumerate(ORDER))
+        return i, j
+
+    def place_of(t):
+        i, j = steps_of(t // NZ)
         return mod4(x + i), mod4(y + j), lax.rem(t, NZ)
 
     def load(t):
@@ -339,32 +354,45 @@
     places[leaf] = place
     pl.semaphore_wait(barrier, greeted)
 
-    def share(k):
-        return pltpu.make_async_remote_copy(
+    def share(pair, z):
+        i, j = steps_of(pair)
+        to = (z * NY + mod4(y - j)) * NX + mod4(x - i)
+        copy = pltpu.make_async_remote_copy(
             src_ref=places.at[leaf],
             dst_ref=places.at[leaf],
-            send_sem=place_send.at[k - 1],
-            recv_sem=place_recv.at[k - 1],
-            device_id=peer(k),
+            send_sem=place_send.at[NZ * pair + z],
+            recv_sem=place_recv.at[NZ * pair + zh],
+            device_id={"leaf": to},
             device_id_type=pl.DeviceIdType.MESH,
         )
-
-    def share_start(k, carry):
-        share(k).start()
+        return to, copy
+
+    def share_start(pair, carry):
+        for z in range(NZ):
+            to, copy = share(pair, z)
+            pl.when(to != leaf)(copy.start)
         return carry
 
-    def share_arrived(k, carry):
-        share(k).wait_recv()
+    def share_sent(pair, carry):
+        for z in range(NZ):
+            to, copy = share(pair, z)
+            pl.when(to != leaf)(copy.wait_send)
         return carry
 
-    def share_sent(k, carry):
-        share(k).wait_send()
-        return carry
-
-    lax.fori_loop(1, GROUP, share_start, 0)
+    def share_arrived(pair, z, dest):
+        copy = pltpu.make_async_remote_copy(
+            src_ref=places.at[dest],
+            dst_ref=places.at[dest],
+            send_sem=place_send.at[NZ * pair + z],
+            recv_sem=place_recv.at[NZ * pair + z],
+            device_id={"leaf": dest},
+            device_id_type=pl.DeviceIdType.MESH,
+        )
+        pl.when(dest != leaf)(copy.wait_recv)
+
+    lax.fori_loop(0, len(ORDER), share_start, 0)
     node_pick = selection(leaf_order(node_skel[pl.ds(node, 1), :]))[:RANK].astype(BF16)
     unpick[...] = selection(place).T
-    lax.fori_loop(1, GROUP, share_arrived, 0)
 
     halves = []
     rest = list(rest)
@@ -392,67 +420,88 @@
             )
         halves.append(pair)
 
-    def multiply(t, carry):
-        xd, yd, zd = place_of(t)
-        dest = (zd * NY + yd) * NX + xd
-        slot = lax.rem(t, SLOTS)
-        load(t).wait()
+    def multiply(pair, carry):
+        i, j = steps_of(pair)
+        xd, yd = mod4(x + i), mod4(y + j)
         rows_iota = lax.broadcasted_iota(jnp.int32, (LR, LR), 0).astype(F32)
-        pick = (rows_iota == places[dest]).astype(F32).astype(BF16)
-        for b in range(probes.shape[0] // LR):
-            cols = pl.ds(b * LR, LR)
-            moved = jnp.dot(pick, slots[slot, :, cols], preferred_element_type=F32)
-            own = leaf * (probes.shape[0] // LR) + b == grp * (NX * NY * NZ) + dest
-            permuted[:, cols] = jnp.where(own, 0.0, moved).astype(BF16)
+        for zd in range(NZ):
+            t = NZ * pair + zd
+            dest = (zd * NY + yd) * NX + xd
+            slot = lax.rem(t, SLOTS)
+            load(t).wait()
+            share_arrived(pair, zd, dest)
+            pick = (rows_iota == places[dest]).astype(F32).astype(BF16)
+            for block in range(probes.shape[0] // LR):
+                cols = pl.ds(block * LR, LR)
+                moved = jnp.dot(pick, slots[slot, :, cols], preferred_element_type=F32)
+                own = leaf * (probes.shape[0] // LR) + block == grp * GROUP + dest
+                permuted[zd, :, cols] = jnp.where(own, 0.0, moved).astype(BF16)
         for h in range(2):
-            product = jnp.dot(
-                permuted[...], probes[:, pl.ds(h * HALF, HALF)], preferred_element_type=F32
-            )
-            for c, (row, rows, z_first) in enumerate(CHUNKS):
-                at = (xd, yd) if h == 0 else (yd, xd)
-                at = (zd, *at) if z_first else (*at, zd)
-                halves[c][h].whole[at] = product[row : row + rows]
-
-        @pl.when(t + SLOTS < NX * NY * NZ)
+            for zd in range(NZ):
+                product = jnp.dot(
+                    permuted[zd], probes[:, pl.ds(h * HALF, HALF)], preferred_element_type=F32
+                )
+                for c, (row, rows, z_first) in enumerate(CHUNKS):
+                    at = (xd, yd) if h == 0 else (yd, xd)
+                    at = (zd, *at) if z_first else (*at, zd)
+                    halves[c][h].whole[at] = product[row : row + rows]
+
+        @pl.when(NZ * pair + SLOTS < GROUP)
         def _():
-            load(t + SLOTS).start()
+            for zd in range(NZ):
+                load(NZ * pair + zd + SLOTS).start()
 
         return carry
 
-    a, b, d = halves
+    a, e, b, d = halves
     xs = [(k, mod4(x + k)) for k in range(4)]
-    lax.fori_loop(0, 8, multiply, 0)
-    a[0].start(0, OPP_R, OPP_L)
-    for h in range(2):
-        d[h].z_start(xs[2])
-    lax.fori_loop(8, 14, multiply, 0)
-    a[1].start(0, OPP_R, OPP_L)
-    lax.fori_loop(14, 20, multiply, 0)
+
+    def z_parts(k):
+        for h in range(2):
+            d[h].z_start(xs[k])
+
+    lax.fori_loop(0, 4, multiply, 0)
+    for part in (a, e):
+        part[0].start(0, OPP_R, OPP_L)
+    z_parts(2)
+    lax.fori_loop(4, 7, multiply, 0)
+    for part in (a, e):
+        part[1].start(0, OPP_R, OPP_L)
+    lax.fori_loop(7, 10, multiply, 0)
     a[0].start(0, NEAR_RB)
-    for h in range(2):
-        d[h].z_start(xs[1])
-    lax.fori_loop(20, 26, multiply, 0)
+    z_parts(1)
+    lax.fori_loop(10, 13, multiply, 0)
     a[0].start(0, NEAR_LA)
-    for h in range(2):
-        d[h].z_start(xs[3])
-    lax.fori_loop(26, 32, multiply, 0)
+    a[0].relay(0)
+    e[0].start(0, NEAR_RB, NEAR_LA)
+    z_parts(3)
+    lax.fori_loop(13, 16, multiply, 0)
     a[1].start(0, NEAR_RB, NEAR_LA)
-    for h in range(2):
-        d[h].z_start(xs[0])
-    for h in range(2):
-        a[h].relay(0)
+    a[1].relay(0)
+    e[1].start(0, NEAR_RB, NEAR_LA)
+    z_parts(0)
     for h in range(2):
         a[h].gather(0)
         a[h].start(1, OPP_R, OPP_L, NEAR_RB, NEAR_LA)
     for h in range(2):
+        e[h].relay(0)
+    for h in range(2):
+        a[h].relay(1)
+    for h in range(2):
+        e[h].gather(0)
+        e[h].start(1, OPP_R, OPP_L, NEAR_RB, NEAR_LA)
+    for h in range(2):
         b[h].start(0, OPP_R, OPP_L)
-    for h in range(2):
-        a[h].relay(1)
-    for h in range(2):
-        b[h].start(0, NEAR_RB, NEAR_LA)
     for h in range(2):
         a[h].gather(1)
         a[h].z_start()
+    for h in range(2):
+        e[h].relay(1)
+    for h in range(2):
+        b[h].start(0, NEAR_RB, NEAR_LA)
+    for h in range(2):
+        e[h].gather(1)
+        e[h].z_start()
     for h in range(2):
         b[h].relay(0)
 
@@ -467,10 +516,9 @@
         )
 
     for h in range(2):
-        rows = a[h].finish()
+        rows = jnp.concatenate([a[h].finish(), e[h].finish()], 0)
         for c in range(2 * h, 2 * h + 2):
-            piece = rows[:, (c - 2 * h) * PIECE : (c - 2 * h + 1) * PIECE]
-            leaf_rows[c] = piece
+            leaf_rows[c] = rows[:, (c - 2 * h) * PIECE : (c - 2 * h + 1) * PIECE]
 
             @pl.when(odd)
             def _():
@@ -573,7 +621,7 @@
         def _():
             climb(node_rows, c, side, 2, 0).wait_send()
 
-    lax.fori_loop(1, GROUP, share_sent, 0)
+    lax.fori_loop(0, len(ORDER), share_sent, 0)
     for pair in halves:
         for half in pair:
             for copy in half.started:
@@ -584,7 +632,7 @@
     depth = probes.shape[0]
     scratch = [
         pltpu.VMEM((SLOTS, LR, depth), BF16),
-        pltpu.VMEM((LR, depth), BF16),
+        pltpu.VMEM((NZ, LR, depth), BF16),
         pltpu.VMEM((GROUP, 1, LR), F32),
         pltpu.VMEM((PIECES, RANK, PIECE), F32),
         pltpu.VMEM((PIECES, RANK, PIECE), F32),
@@ -592,8 +640,8 @@
         pltpu.VMEM((LR, LR), F32),
         pltpu.VMEM((PIECES, RANK, PIECE), F32),
         pltpu.SemaphoreType.DMA((SLOTS,)),
-        pltpu.SemaphoreType.DMA((GROUP - 1,)),
-        pltpu.SemaphoreType.DMA((GROUP - 1,)),
+        pltpu.SemaphoreType.DMA((GROUP,)),
+        pltpu.SemaphoreType.DMA((GROUP,)),
         pltpu.SemaphoreType.DMA((3, PIECES)),
         pltpu.SemaphoreType.DMA((2, PIECES)),
         pltpu.SemaphoreType.DMA((len(CHUNKS), 2, N_COPY)),

time: 145 us -> 136 us (0.938)
  Pallas kernels: 142 us -> 132 us
    pallas_call x1, Pallas kernels: 142 us -> 132 us  [bases(): pl.pallas_call(kernel, out_shape=(jax.ShapeDtypeStruct((LR, RANK), F32),...]
where the time goes in v5:
time: 136 us
  Pallas kernels  132 us (97%)
  local copies, waits for them, and re-layouts  3.14 us (2%)
    pallas_call x1, Pallas kernels, bases(): pl.pallas_call(kernel, out_shape=(jax.ShapeDtypeStruct((LR, RANK), F32),...  132 us
    unnamed x2, local copies, waits for them, and re-layouts  3.14 us

profile of v5, /device:TPU:0, one launch (start us, length us, event | category | flops | bytes accessed | tf_op | source)
XLA Modules:
  0.0 136.1 jit_solution(7690115680608831065)
XLA Ops:
  0.6 132.3 %bases.1 = (f32[256,128]{1,0:T(8,128)}, f32[1,256,128]{2,1,0:T(8,128)}) custom-call(bf16[8192,1024]{1,0:T(8,128)(2,1)} %matrix.1, bf16[1024,512]{1,0:T(8,128)(2,1)} %probes.1, s32[1,128]{1,0:T(1,128)} %skel.1, s32[127,128]{1,0:T(8,128)} %node_skel.1), custom_call_target="tpu_custom_call" | custom-call | tf_op jit(solution)/shard_map/bases/pallas_call | solution.py:664
  132.9 1.6 %copy.8 = f32[256,128]{1,0:T(8,128)} copy(f32[256,128]{1,0:T(8,128)} %get-tuple-element.4) | data formatting | bytes 262144
  134.5 1.6 %copy.9 = f32[1,256,128]{2,1,0:T(8,128)} copy(f32[1,256,128]{2,1,0:T(8,128)} %get-tuple-element.5) | data formatting | bytes 262144

commit v6 on v5

--- a/solution.py
+++ b/solution.py
@@ -25,13 +25,14 @@
     [(2, 0), (2, 1), (2, 2), (2, 3)]
     + [(0, 2), (1, 2), (3, 2)]
     + [(1, 0), (1, 1), (1, 3)]
-    + [(3, 0), (3, 1), (3, 3)]
-    + [(0, 1), (0, 3), (0, 0)]
+    + [(0, 1), (3, 1)]
+    + [(3, 0), (3, 3)]
+    + [(0, 3), (0, 0)]
 )
 OPP_R, OPP_L, NEAR_RA, NEAR_RB, NEAR_LA, NEAR_LB = range(6)
 PASS = 6
 Z_COPY = 2 * PASS
-N_COPY = 2 * PASS + 4
+N_COPY = 2 * PASS + 12
 
 
 def mod4(v):
@@ -49,6 +50,7 @@
         self.zh = zh
         self.dev = dev
         self.started = []
+        self.pieces = False
 
     def block(self, phase, index):
         if phase == 0:
@@ -94,12 +96,39 @@
             self.dev(**{name: to}),
         )
 
+    def piece(self, kind, other):
+        name, me = self.axes[0]
+        half = self.rows // 2
+        return self.remote(
+            self.part.at[mod4(me + 2), other, :, pl.ds(kind * half, half)],
+            self.bufs[0][0].at[kind, other],
+            2 * PASS + 4 + 4 * kind + other,
+            self.dev(**{name: mod4(me + 1) if kind == OPP_R else mod4(me - 1)}),
+        )
+
+    def piece_start(self, other):
+        self.pieces = True
+        for kind in (OPP_R, OPP_L):
+            self.piece(kind, other).start()
+
     def start(self, phase, *kinds):
         for kind in kinds:
             self.begin(self.copy(phase, kind))
 
     def wait(self, phase, kind):
-        self.copy(phase, kind).wait_recv()
+        if phase == 0 and self.pieces and kind in (OPP_R, OPP_L):
+            for other in range(4):
+                self.piece(kind, other).wait_recv()
+        else:
+            self.copy(phase, kind).wait_recv()
+
+    def wait_sent(self):
+        for copy in self.started:
+            copy.wait_send()
+        if self.pieces:
+            for kind in (OPP_R, OPP_L):
+                for other in range(4):
+                    self.piece(kind, other).wait_send()
 
     def relay(self, phase):
         me = self.axes[phase][1]
@@ -260,7 +289,7 @@
     node_rows,
     stack,
     unpick,
-    weights,
+    leaf_cross,
     in_sem,
     place_send,
     place_recv,
@@ -460,23 +489,34 @@
         for h in range(2):
             d[h].z_start(xs[k])
 
-    lax.fori_loop(0, 4, multiply, 0)
-    for part in (a, e):
-        part[0].start(0, OPP_R, OPP_L)
+    def along_y(pair, carry):
+        multiply(pair, carry)
+        a[0].piece_start(mod4(y + steps_of(pair)[1]))
+        return carry
+
+    def along_x(pair, carry):
+        multiply(pair, carry)
+        a[1].piece_start(mod4(x + steps_of(pair)[0]))
+        return carry
+
+    lax.fori_loop(0, 4, along_y, 0)
+    e[0].start(0, OPP_R, OPP_L)
+    a[1].piece_start(mod4(x + 2))
     z_parts(2)
-    lax.fori_loop(4, 7, multiply, 0)
-    for part in (a, e):
-        part[1].start(0, OPP_R, OPP_L)
+    lax.fori_loop(4, 7, along_x, 0)
+    e[1].start(0, OPP_R, OPP_L)
     lax.fori_loop(7, 10, multiply, 0)
     a[0].start(0, NEAR_RB)
     z_parts(1)
-    lax.fori_loop(10, 13, multiply, 0)
+    lax.fori_loop(10, 12, multiply, 0)
+    a[1].start(0, NEAR_RB)
+    lax.fori_loop(12, 14, multiply, 0)
     a[0].start(0, NEAR_LA)
     a[0].relay(0)
     e[0].start(0, NEAR_RB, NEAR_LA)
     z_parts(3)
-    lax.fori_loop(13, 16, multiply, 0)
-    a[1].start(0, NEAR_RB, NEAR_LA)
+    lax.fori_loop(14, 16, multiply, 0)
+    a[1].start(0, NEAR_LA)
     a[1].relay(0)
     e[1].start(0, NEAR_RB, NEAR_LA)
     z_parts(0)
@@ -551,61 +591,65 @@
                 def _():
                     climb(node_rows, c, side, 2, 0).start()
 
-    def gram_of(rows):
-        gram = 0.0
+    def cross_of(rows, against):
+        cross = 0.0
         for c in range(PIECES):
-            gram = gram + times_transposed(rows[c], rows[c])
-        return gram
-
-    tree(1, 2)
+            cross = cross + times_transposed(rows(c), against[c])
+        return cross
+
+    def add_crosses(row, parts):
+        crosses = []
+        for part in parts:
+            halves = [part[h].finish() for h in range(2)]
+            crosses.append(
+                cross_of(
+                    lambda c: halves[c // 2][:, (c % 2) * PIECE : (c % 2 + 1) * PIECE], leaf_rows
+                )
+            )
+        cross = jnp.concatenate(crosses, 0)
+        pick = unpick[:, row : row + cross.shape[0]].astype(BF16)
+        leaf_cross[...] += select(pick, cross)
+
+    first_all = (OPP_R, OPP_L, NEAR_RB, NEAR_LA)
+    tree(1, 1)
+    d[1].z_merge(xs)
+    d[1].start(0, *first_all)
+    tree(2, 2)
     for h in range(2):
         b[h].gather(0)
-        b[h].start(1, OPP_R, OPP_L, NEAR_RB, NEAR_LA)
+        b[h].start(1, *first_all)
+    d[1].relay(0)
     tree(3, 3)
     for h in range(2):
         b[h].relay(1)
+    d[0].z_merge(xs)
+    d[0].start(0, *first_all)
+    d[1].gather(0)
+    d[1].start(1, *first_all)
     tree(4, 4)
-    for h in range(2):
-        d[h].z_merge(xs)
-        d[h].start(0, OPP_R, OPP_L, NEAR_RB, NEAR_LA)
-    tree(5, 5)
+    d[0].relay(0)
     for h in range(2):
         b[h].gather(1)
         b[h].z_start()
-    for h in range(2):
-        d[h].relay(0)
+    tree(5, 5)
+    d[1].relay(1)
+    d[0].gather(0)
+    d[0].start(1, *first_all)
     tree(6, 6)
-    for h in range(2):
-        d[h].gather(0)
-        d[h].start(1, OPP_R, OPP_L, NEAR_RB, NEAR_LA)
+    d[0].relay(1)
+    leaf_gram = cross_of(lambda c: leaf_rows[c], leaf_rows)
+    leaf_cross[...] = select(unpick[:, :RANK].astype(BF16), leaf_gram)
     tree(7, 7)
-    for h in range(2):
-        d[h].relay(1)
-    leaf_inv, node_inv = inverses((gram_of(leaf_rows), gram_of(node_rows)))
-    known = 0.0
-    basis = 0.0
-    for c in range(PIECES):
-        weight = jnp.dot(leaf_inv, leaf_rows[c], precision=HIGHEST, preferred_element_type=F32)
-        weights[c] = weight
-        known = known + times_transposed(leaf_rows[c], weight)
-        weight = jnp.dot(node_inv, node_rows[c], precision=HIGHEST, preferred_element_type=F32)
-        basis = basis + times_transposed(stack[c].reshape(LR, PIECE), weight)
-    node_out[0] = basis
-    leaf_out[...] = select(unpick[:, :RANK].astype(BF16), known)
-
-    found = []
-    for part in (b, d):
-        basis = 0.0
-        for h in range(2):
-            if part is d:
-                part[h].gather(1)
-            rows = part[h].finish()
-            for c in range(2):
-                basis = basis + times_transposed(
-                    rows[:, c * PIECE : (c + 1) * PIECE], weights[2 * h + c]
-                )
-        found.append(basis)
-    leaf_out[...] += select(unpick[:, RANK:].astype(BF16), jnp.concatenate(found, 0))
+    node_cross = cross_of(lambda c: stack[c].reshape(LR, PIECE), node_rows)
+    node_gram = select(node_pick, node_cross)
+    for h in range(2):
+        d[h].gather(1)
+    add_crosses(RANK, (b, d))
+    leaf_inv, node_inv = inverses((leaf_gram, node_gram))
+    node_out[0] = jnp.dot(node_cross, node_inv, precision=HIGHEST, preferred_element_type=F32)
+    leaf_out[...] = jnp.dot(
+        leaf_cross[...], leaf_inv, precision=HIGHEST, preferred_element_type=F32
+    )
 
     for c in range(PIECES):
 
@@ -624,8 +668,7 @@
     lax.fori_loop(0, len(ORDER), share_sent, 0)
     for pair in halves:
         for half in pair:
-            for copy in half.started:
-                copy.wait_send()
+            half.wait_sent()
 
 
 def bases(matrix, probes, skel, node_skel):
@@ -638,7 +681,7 @@
         pltpu.VMEM((PIECES, RANK, PIECE), F32),
         pltpu.VMEM((PIECES, 2, RANK, PIECE), F32),
         pltpu.VMEM((LR, LR), F32),
-        pltpu.VMEM((PIECES, RANK, PIECE), F32),
+        pltpu.VMEM((LR, RANK), F32),
         pltpu.SemaphoreType.DMA((SLOTS,)),
         pltpu.SemaphoreType.DMA((GROUP,)),
         pltpu.SemaphoreType.DMA((GROUP,)),

time: 136 us -> 134 us (0.985)
  Pallas kernels: 132 us -> 130 us
    pallas_call x1, Pallas kernels: 132 us -> 130 us  [bases(): pl.pallas_call(kernel, out_shape=(jax.ShapeDtypeStruct((LR, RANK), F32),...]
where the time goes in v6:
time: 134 us
  Pallas kernels  130 us (97%)
  local copies, waits for them, and re-layouts  3.14 us (2%)
    pallas_call x1, Pallas kernels, bases(): pl.pallas_call(kernel, out_shape=(jax.ShapeDtypeStruct((LR, RANK), F32),...  130 us
    unnamed x2, local copies, waits for them, and re-layouts  3.14 us

profile of v6, /device:TPU:0, one launch (start us, length us, event | category | flops | bytes accessed | tf_op | source)
XLA Modules:
  0.0 133.8 jit_solution(15215456517070319431)
XLA Ops:
  0.6 130.0 %bases.1 = (f32[256,128]{1,0:T(8,128)}, f32[1,256,128]{2,1,0:T(8,128)}) custom-call(bf16[8192,1024]{1,0:T(8,128)(2,1)} %matrix.1, bf16[1024,512]{1,0:T(8,128)(2,1)} %probes.1, s32[1,128]{1,0:T(1,128)} %skel.1, s32[127,128]{1,0:T(8,128)} %node_skel.1), custom_call_target="tpu_custom_call" | custom-call | tf_op jit(solution)/shard_map/bases/pallas_call | solution.py:707
  130.7 1.6 %copy.8 = f32[256,128]{1,0:T(8,128)} copy(f32[256,128]{1,0:T(8,128)} %get-tuple-element.4) | data formatting | bytes 262144
  132.2 1.6 %copy.9 = f32[1,256,128]{2,1,0:T(8,128)} copy(f32[1,256,128]{2,1,0:T(8,128)} %get-tuple-element.5) | data formatting | bytes 262144

commit v7 on v6

--- a/solution.py
+++ b/solution.py
@@ -464,15 +464,16 @@
                 cols = pl.ds(block * LR, LR)
                 moved = jnp.dot(pick, slots[slot, :, cols], preferred_element_type=F32)
                 own = leaf * (probes.shape[0] // LR) + block == grp * GROUP + dest
-                permuted[zd, :, cols] = jnp.where(own, 0.0, moved).astype(BF16)
+                permuted[pl.ds(zd * LR, LR), cols] = jnp.where(own, 0.0, moved).astype(BF16)
         for h in range(2):
+            product = jnp.dot(
+                permuted[...], probes[:, pl.ds(h * HALF, HALF)], preferred_element_type=F32
+            )
             for zd in range(NZ):
-                product = jnp.dot(
-                    permuted[zd], probes[:, pl.ds(h * HALF, HALF)], preferred_element_type=F32
-                )
                 for c, (row, rows, z_first) in enumerate(CHUNKS):
                     at = (xd, yd) if h == 0 else (yd, xd)
                     at = (zd, *at) if z_first else (*at, zd)
+                    row += zd * LR
                     halves[c][h].whole[at] = product[row : row + rows]
 
         @pl.when(NZ * pair + SLOTS < GROUP)
@@ -675,7 +676,7 @@
     depth = probes.shape[0]
     scratch = [
         pltpu.VMEM((SLOTS, LR, depth), BF16),
-        pltpu.VMEM((NZ, LR, depth), BF16),
+        pltpu.VMEM((NZ * LR, depth), BF16),
         pltpu.VMEM((GROUP, 1, LR), F32),
         pltpu.VMEM((PIECES, RANK, PIECE), F32),
         pltpu.VMEM((PIECES, RANK, PIECE), F32),

time: 134 us -> 134 us (level)
  no operation moved by 1% of the time
where the time goes in v7:
time: 134 us
  Pallas kernels  130 us (97%)
  local copies, waits for them, and re-layouts  3.14 us (2%)
    pallas_call x1, Pallas kernels, bases(): pl.pallas_call(kernel, out_shape=(jax.ShapeDtypeStruct((LR, RANK), F32),...  130 us
    unnamed x2, local copies, waits for them, and re-layouts  3.14 us

profile of v7, /device:TPU:0, one launch (start us, length us, event | category | flops | bytes accessed | tf_op | source)
XLA Modules:
  0.0 133.8 jit_solution(3113407096001491972)
XLA Ops:
  0.6 130.0 %bases.1 = (f32[256,128]{1,0:T(8,128)}, f32[1,256,128]{2,1,0:T(8,128)}) custom-call(bf16[8192,1024]{1,0:T(8,128)(2,1)} %matrix.1, bf16[1024,512]{1,0:T(8,128)(2,1)} %probes.1, s32[1,128]{1,0:T(1,128)} %skel.1, s32[127,128]{1,0:T(8,128)} %node_skel.1), custom_call_target="tpu_custom_call" | custom-call | tf_op jit(solution)/shard_map/bases/pallas_call | solution.py:708
  130.6 1.6 %copy.8 = f32[256,128]{1,0:T(8,128)} copy(f32[256,128]{1,0:T(8,128)} %get-tuple-element.4) | data formatting | bytes 262144
  132.2 1.6 %copy.9 = f32[1,256,128]{2,1,0:T(8,128)} copy(f32[1,256,128]{2,1,0:T(8,128)} %get-tuple-element.5) | data formatting | bytes 262144
